TPU v7x, 128 devices: a whole 4x4x4 slice. The times are simulated.
128 devices in a mesh: row: 8 (over z, core), col: 16 (over y, x).
Axes of the slice: x: 4, y: 4, z: 4, core: 2. Of those that a mesh axis runs over, the one named last changes fastest.
Arguments:
- amplitudes: float32 [2048, 8192], P('col', 'row'), may hold values from -6 to 6
- integral_tiles: float32 [128, 128, 1, 128, 128], P(None, ('row', 'col')), may hold values from -0.09375 to 0.09375
- integral_blocks: int32 [128, 128, 1, 2], P(None, ('row', 'col')), may hold values from -1 to 511, as said below
Outputs:
- pair_ladder: float32 [2048, 65536], P('row', 'col')
Inputs may be any that keep to these rules, and one draw needn't show every extreme that they name: `integral_blocks`: take a device g of the mesh over row+col (row slowest) with row index r and column index c. Entries [g, d, s, :] describe position j = d + s of the 128 listed tiles of g, held by device d. The positions form 4 groups of 32 in a row; in a live group, position j holds cd tile r * 8 + u, with u the same within the group and different between groups, and ab tile c * 32 + (j mod 32); in an empty group both entries are -1. Live groups come first; a quarter of 4 or more are live on every g, and all 4 on some g. Cd tiles lie below 8 * 8 and ab tiles below 32 * 16.
All inputs are finite; a program needn't handle non-finite values.
Results may differ from a plain program's by a relative error of at most 0.0003.
Values sent between devices are 32-bit elements; how exact they have to be, the bound alone decides.
No kernel may reach another device: no remote copies, remote signals or barrier semaphores. Data moves between devices by JAX's collectives and lax.ppermute only.
A program may use at most 128 MiB of HBM per device.

v0:
```python
import jax
import jax.numpy as jnp
from jax import lax
from jax.sharding import PartitionSpec as P

TB = 128
ABT = 32
CD_ROW = 8
GROUPS = 4


def per_device(amplitudes, integral_tiles, integral_blocks):
    tiles_here, coords_here = (
        lax.all_to_all(integral_tiles, ("row", "col"), split_axis=0, concat_axis=1, tiled=True),
        lax.all_to_all(integral_blocks, ("row", "col"), split_axis=0, concat_axis=1, tiled=True),
    )
    tile_groups = tiles_here.reshape(GROUPS, ABT, TB, TB)
    coord_list = coords_here.reshape(GROUPS * ABT, 2)
    group_cd = coord_list[::ABT, 0]
    present = group_cd >= 0
    local_cd = jnp.where(present, group_cd % CD_ROW, 0).astype(jnp.int32)
    weight = present.astype(jnp.float32)
    gathered = lax.all_gather(amplitudes, "col", axis=0, tiled=True)
    chosen = jnp.take(gathered.reshape(gathered.shape[0], CD_ROW, TB), local_cd, axis=1)
    chosen = chosen * weight[None, :, None]
    all_pairs = chosen.shape[0]
    product = jnp.einsum("pqx,qaxy->pay", chosen, tile_groups, precision=lax.Precision.HIGHEST)
    return lax.psum_scatter(
        product.reshape(lax.axis_size("row") * (all_pairs // lax.axis_size("row")), ABT * TB),
        "row",
        scatter_dimension=0,
        tiled=True,
    )


def solution(mesh):
    placed = (
        P("col", "row"),
        P(None, ("row", "col"), None, None, None),
        P(None, ("row", "col"), None, None),
    )
    return jax.shard_map(
        per_device, mesh=mesh, in_specs=placed, out_specs=P("row", "col"), check_vma=False
    )
```

profile of v0, /device:TPU:3, one launch (start us, length us, event | category | flops | bytes accessed | tf_op | source)
XLA Modules:
  0.0 436.5 jit_solution(10573017534802516923)
XLA Ops:
  6.5 0.0 all-gather.2.cloned.1.call-start
  6.5 2.0 copy.14
  8.6 0.0 all-gather.2.cloned.1.call-update
  8.6 0.8 copy.13
  9.4 19.1 %all_to_all.8 = s32[128,1,1,2]{3,2,1,0:T(1,128)S(1)} all-to-all(s32[128,1,1,2]{3,2,1,0:T(1,128)S(1)} %copy.13), channel_id=1, replica_groups=mesh['row'=8,'col'=16] {'row','col'}, dimensions={0} | all-to-all | bytes 2048 | tf_op jit(solution)/shard_map/all_to_all | solution.py:15
  28.5 6.7 %all-to-all-start.1 = ((f32[128,1,1,128,128]{4,3,2,1,0:T(8,128)}), f32[128,1,1,128,128]{4,3,2,1,0:T(8,128)}, u32[]{:S(2)}, u32[]{:S(2)}) async-start(f32[128,1,1,128,128]{4,3,2,1,0:T(8,128)} %param.4), calls=%async_computation.1 | async-start | bytes 16777216 | tf_op jit(solution)/shard_map/all_to_all | solution.py:14
  35.3 0.0 reduce-scatter.2.cloned.1.call-start
  35.3 0.1 and_reduce_fusion
  35.5 0.1 reduce.1
  35.6 0.1 convert_reduce_fusion
  35.7 139.4 %all-to-all-done.1 = f32[128,1,1,128,128]{4,3,2,1,0:T(8,128)} async-done(((f32[128,1,1,128,128]{4,3,2,1,0:T(8,128)}), f32[128,1,1,128,128]{4,3,2,1,0:T(8,128)}, u32[]{:S(2)}, u32[]{:S(2)}) %all-to-all-start.1) | async-done | bytes 8388640 | tf_op jit(solution)/shard_map/all_to_all | solution.py:14
  175.2 8.9 %copy.16 = f32[4,32,128,128]{2,3,1,0:T(8,128)} copy(f32[4,32,128,128]{3,2,1,0:T(8,128)} %bitcast.3) | data formatting | bytes 16777216 | tf_op jit(solution)/shard_map/reshape | solution.py:17
  184.1 0.0 all-gather.2.cloned.1.call-done
  184.1 9.1 %copy.15 = f32[2048,8,128]{2,0,1:T(8,128)} copy(f32[2048,8,128]{0,2,1:T(8,128)} %bitcast.16) | data formatting | bytes 16777216 | tf_op jit(solution)/shard_map/reshape | solution.py:24
  193.2 6.2 %gather_fusion = f32[4,2048,128]{2,1,0:T(8,128)} fusion(f32[2048,8,128]{2,0,1:T(8,128)} %copy.15, s32[1024]{0:T(1024)S(1)} %pad_clamp_fusion), kind=kCustom, calls=%fused_computation | custom fusion | bytes 8388624 | tf_op jit(solution)/shard_map/jit(_take)/gather | solution.py:24
  199.4 59.5 %convolution_bitcast_fusion = f32[2048,4096]{1,0:T(8,128)} fusion(f32[4096,4,128]{2,0,1:T(8,128)} %bitcast.17, f32[4,2048,128]{2,1,0:T(8,128)} %gather_fusion, f32[4]{0:T(128)S(1)} %convert_reduce_fusion, pred[4]{0:T(512)(128)(4,1)S(1)} %get-tuple-element.5), kind=kOutput, calls=%fused_computation.1 | convolution fusion | flops 51541704704 | bytes 46137364 | tf_op jit(solution)/shard_map/pqx,qaxy->pay/dot_general | solution.py:27
  258.9 0.0 reduce-scatter.2.cloned.1.call-update
  259.0 170.7 %reduce-scatter.2.cloned.1.call-done = f32[256,4096]{1,0:T(8,128)} async-done(((f32[2048,4096]{1,0:T(8,128)}), f32[256,4096]{1,0:T(8,128)}) %reduce-scatter.2.cloned.1.call-update) | async-done | bytes 4194320 | tf_op jit(solution)/shard_map/reduce_scatter | solution.py:28
  (2 shorter events, 0.0 us)
Async XLA Ops:
  6.5 177.6 %all-gather.2.cloned.1.call-start = ((), (), s32[]{:S(2)}) async-start(), calls=%async_computation.3 | async-start | bytes 8912896 | tf_op jit(solution)/shard_map/all_gather | solution.py:23
  28.5 146.6 %all-to-all-start.1 = ((f32[128,1,1,128,128]{4,3,2,1,0:T(8,128)}), f32[128,1,1,128,128]{4,3,2,1,0:T(8,128)}, u32[]{:S(2)}, u32[]{:S(2)}) async-start(f32[128,1,1,128,128]{4,3,2,1,0:T(8,128)} %param.4), calls=%async_computation.1 | async-start | bytes 16777216 | tf_op jit(solution)/shard_map/all_to_all | solution.py:14
  35.3 394.4 %reduce-scatter.2.cloned.1.call-start = ((), (), s32[]{:S(2)}) async-start(), calls=%async_computation.4 | async-start | bytes 37748736 | tf_op jit(solution)/shard_map/reduce_scatter | solution.py:28
Sparse Core Ops, SparseCore 0:
  9.5 168.7 all-gather.1
  259.1 170.5 reduce-scatter.1
where the time goes:
time: 438 us; the launch traced here: 437 us
  waiting for transfers between devices  310 us (71%)
  matrix products  59.5 us (14%)
  local copies, waits for them, and re-layouts  27.1 us (6%)
  blocking collectives  19.1 us (4%)
  between operations  13.4 us (3%)
  starting transfers between devices  6.77 us (2%)
    reduce_scatter x1, waiting for transfers between devices, per_device(): lax.psum_scatter(product.reshape(lax.axis_size('row') * (all_pairs // lax...  171 us
    all_to_all x1, waiting for transfers between devices, per_device(): lax.all_to_all(integral_tiles, ('row', 'col'), split_axis=0, concat_axis=...  139 us
    dot_general x1, matrix products, per_device(): jnp.einsum('pqx,qaxy->pay', chosen, tile_groups, precision=lax.Precision....  59.5 us
    all_to_all x1, blocking collectives, per_device(): lax.all_to_all(integral_blocks, ('row', 'col'), split_axis=0, concat_axis...  19.1 us
    reshape x1, local copies, waits for them, and re-layouts, per_device(): gathered.reshape(gathered.shape[0], CD_ROW, TB)  9.12 us
    reshape x1, local copies, waits for them, and re-layouts, per_device(): tile_groups = tiles_here.reshape(GROUPS, ABT, TB, TB)  8.95 us
  transfers between devices with their start and end apart: 3, of which 2 were waited for; matrix products, arithmetic and copies ran while one was open for 2% of the time, Pallas kernels for 0%

commit v1 on v0

v1 whole, which is shorter than its diff:
```python
import jax
import jax.numpy as jnp
from jax import lax
from jax.experimental import pallas as pl
from jax.experimental.pallas import tpu as pltpu
from jax.sharding import PartitionSpec as P

TB = 128
ABT = 32
CD_ROW = 8
SIDE = 4
N_ROW = 8
N_COL = 16
HALF = 256
PLANE = 512
GCOLS = SIDE * TB
ANYWHERE = ("row", "col")


def col_of(core, a1, a2):
    return jnp.where(core == 0, a2 * SIDE + a1, a1 * SIDE + a2)


def z_shift(step):
    return [(r, ((r // 2 + step) % SIDE) * 2 + r % 2) for r in range(N_ROW)]


def plane_shift(first, step):
    pairs = []
    for r in range(N_ROW):
        for c in range(N_COL):
            y, x = c // SIDE, c % SIDE
            if (r % 2 == 0) == first:
                x = (x + step) % SIDE
            else:
                y = (y + step) % SIDE
            pairs.append((r * N_COL + c, r * N_COL + y * SIDE + x))
    return pairs


def after(values, *deps):
    return lax.optimization_barrier((values, deps))[0]


OTHER_CORE = [(r, r ^ 1) for r in range(N_ROW)]


def params(mib):
    return pltpu.CompilerParams(
        dimension_semantics=("arbitrary",), vmem_limit_bytes=mib * 1024 * 1024
    )


SMALL = pl.CostEstimate(flops=0, bytes_accessed=1024, transcendentals=0)
BIG_MIB, SMALL_MIB = 56, 24


def call(body, grid, table, args, in_specs, out_shape, out_specs, name, mib=BIG_MIB, **more):
    scratch = more.pop("scratch_shapes", [])
    return pl.pallas_call(
        body,
        out_shape=out_shape,
        grid_spec=pltpu.PrefetchScalarGridSpec(
            num_scalar_prefetch=1,
            grid=(grid,),
            in_specs=in_specs,
            out_specs=out_specs,
            scratch_shapes=scratch,
        ),
        compiler_params=params(mib),
        cost_estimate=SMALL,
        name=name,
        **more,
    )(table, *args)


def f32(*shape):
    return jax.ShapeDtypeStruct(shape, jnp.float32)


def fixed(*shape):
    return pl.BlockSpec(shape, lambda j, table: (0,) * len(shape))


def pick_tiles(tiles, table, cols, rows, count):
    def body(table_ref, tiles_ref, *outs):
        for i in range(count):

            @pl.when(pl.program_id(0) == i)
            def _(out=outs[i]):
                for n in range(N_ROW):
                    out[0, n] = tiles_ref[table_ref[rows + n], 0]

    return call(
        body,
        count,
        table,
        [tiles],
        [pl.BlockSpec((N_ROW, 1, TB, TB), lambda j, table_ref: (0, table_ref[cols + j], 0, 0))],
        [f32(1, N_ROW, TB, TB)] * count,
        [fixed(1, N_ROW, TB, TB)] * count,
        "pick_tiles",
    )


def join_tiles(tiles, table, col, rows, passed):
    def body(table_ref, tiles_ref, *refs):
        ins, out = refs[:-1], refs[-1]

        @pl.when(pl.program_id(0) == 0)
        def _():
            for n in range(N_ROW):
                out[0, n] = tiles_ref[table_ref[rows + n], 0]

        for s in range(1, SIDE):

            @pl.when(pl.program_id(0) == s)
            def _(s=s):
                out[...] = ins[s - 1][...]

    block = (1, N_ROW, TB, TB)
    return call(
        body,
        SIDE,
        table,
        [tiles, *passed],
        [pl.BlockSpec((N_ROW, 1, TB, TB), lambda j, table_ref: (0, table_ref[col], 0, 0))]
        + [fixed(*block)] * len(passed),
        f32(SIDE, N_ROW, TB, TB),
        pl.BlockSpec(block, lambda j, table_ref: (j, 0, 0, 0)),
        "join_tiles",
    )


def choose(panels, table, places, live):
    n_ij = panels[0].shape[0]

    def body(table_ref, *refs):
        c = pl.program_id(0)
        out = refs[SIDE]
        for k in range(SIDE):
            at = pl.multiple_of(table_ref[places + c * SIDE + k] * TB, TB)
            tile = refs[k][:, pl.ds(at, TB)]
            listed = table_ref[live + c * SIDE + k] > 0
            out[0, :, k * TB : (k + 1) * TB] = jnp.where(listed, tile, 0.0)

    return call(
        body,
        N_COL,
        table,
        panels,
        [fixed(*p.shape) for p in panels],
        f32(N_COL, n_ij, SIDE * TB),
        pl.BlockSpec((1, n_ij, SIDE * TB), lambda c, table_ref: (c, 0, 0)),
        "choose",
        SMALL_MIB,
    )


def split(x):
    high = x.astype(jnp.bfloat16)
    return high, (x - high.astype(jnp.float32)).astype(jnp.bfloat16)


def product(a_refs, high_ref, low_ref):
    high, low = split(jnp.concatenate([ref[...] for ref in a_refs], axis=1))
    total = jnp.dot(high, low_ref[...], preferred_element_type=jnp.float32)
    total += jnp.dot(low, high_ref[...], preferred_element_type=jnp.float32)
    return total + jnp.dot(high, high_ref[...], preferred_element_type=jnp.float32)


def amp_specs(amps, steps):
    return [
        pl.BlockSpec((HALF, a.shape[1]), lambda i, table_ref: (table_ref[steps + i], 0))
        for a in amps
    ]


DEPTH = N_ROW * TB
TERM = jax.ShapeDtypeStruct((DEPTH, GCOLS), jnp.bfloat16)


def products_away(table, steps, amps, weights):
    def body(table_ref, *refs):
        a_refs, w_refs = refs[: len(amps)], refs[len(amps) : -4]
        half_up, half_down, high_ref, low_ref = refs[-4:]
        i = pl.program_id(0)

        @pl.when(i == 0)
        def _():
            s = 0
            for ref in w_refs:
                for m in range(ref.shape[0]):
                    high, low = split(ref[m].reshape(DEPTH, TB))
                    high_ref[:, s * TB : (s + 1) * TB] = high
                    low_ref[:, s * TB : (s + 1) * TB] = low
                    s += 1

        total = product(a_refs, high_ref, low_ref)

        @pl.when(i == 0)
        def _():
            half_up[...] = total

        @pl.when(i == 1)
        def _():
            half_down[...] = total

    return call(
        body,
        2,
        table,
        [*amps, *weights],
        amp_specs(amps, steps) + [fixed(*w.shape) for w in weights],
        [f32(HALF, GCOLS)] * 2 + [TERM] * 2,
        [fixed(HALF, GCOLS)] * 2 + [fixed(DEPTH, GCOLS)] * 2,
        "products_away",
    )


def products_next(table, steps, amps, terms, from_down, from_up):
    def body(table_ref, *refs):
        a_refs = refs[: len(amps)]
        high_ref, low_ref, f_ref, g_ref, up, down = refs[len(amps) :]
        i = pl.program_id(0)
        total = product(a_refs, high_ref, low_ref)

        @pl.when(i == 0)
        def _():
            up[...] = total + f_ref[...]

        @pl.when(i == 1)
        def _():
            up[...] = total

        @pl.when(i == 2)
        def _():
            down[...] = total

        @pl.when(i == 3)
        def _():
            down[...] = total + g_ref[...]

    return call(
        body,
        4,
        table,
        [*amps, *terms, from_down, from_up],
        amp_specs(amps, steps) + [fixed(DEPTH, GCOLS)] * 2 + [fixed(HALF, GCOLS)] * 2,
        [f32(PLANE, GCOLS)] * 2,
        [
            pl.BlockSpec((HALF, GCOLS), lambda i, table_ref: (jnp.minimum(i, 1), 0)),
            pl.BlockSpec((HALF, GCOLS), lambda i, table_ref: (jnp.maximum(i - 2, 0), 0)),
        ],
        "products_next",
    )


def write_columns(source, out, table_ref, cols, sems):
    copies = []
    for s in range(SIDE):
        at = pl.multiple_of(table_ref[cols + s] * TB, TB)
        copies.append(
            pltpu.make_async_copy(
                source.at[:, pl.ds(s * TB, TB)], out.at[:, pl.ds(at, TB)], sems.at[s]
            )
        )
        copies[-1].start()
    return copies


def products_here(table, steps, amps, terms, from_down, from_up, cols, result, before):
    more = [] if before is None else [before[0]]

    def body(table_ref, *refs):
        a_refs = refs[: len(amps)]
        high_ref, low_ref, f_ref, g_ref = refs[len(amps) : len(amps) + 4]
        theirs, out, mine, sems = refs[-4:]
        i = pl.program_id(0)
        if before is not None:

            @pl.when(i == 0)
            def _():
                copies = write_columns(refs[len(amps) + 4], out, table_ref, before[1], sems)
                for copy in copies:
                    copy.wait()

        total = product(a_refs, high_ref, low_ref) + (f_ref[...] + g_ref[...])

        @pl.when(i == 0)
        def _():
            theirs[...] = total

        @pl.when(i == 1)
        def _():
            mine[...] = total
            for copy in write_columns(mine, out, table_ref, cols, sems):
                copy.wait()

    block = pl.BlockSpec((HALF, GCOLS), lambda i, table_ref: (lax.rem(table_ref[steps + i], 2), 0))
    args = [*amps, *terms, from_down, from_up, *more]
    specs = (
        amp_specs(amps, steps)
        + [fixed(DEPTH, GCOLS)] * 2
        + [block] * 2
        + [fixed(HALF, GCOLS)] * len(more)
    )
    alias = {}
    if result is not None:
        alias = {1 + len(args): 1}
        args.append(result)
        specs.append(pl.BlockSpec(memory_space=pl.ANY))
    return call(
        body,
        2,
        table,
        args,
        specs,
        [f32(HALF, GCOLS), f32(HALF, ABT * TB)],
        [fixed(HALF, GCOLS), pl.BlockSpec(memory_space=pl.ANY)],
        "products_here",
        input_output_aliases=alias,
        scratch_shapes=[pltpu.VMEM((HALF, GCOLS), jnp.float32), pltpu.SemaphoreType.DMA((SIDE,))],
    )


def place(table, theirs, cols, result):
    def body(table_ref, theirs_ref, result_ref, out, sems):
        for copy in write_columns(theirs_ref, out, table_ref, cols, sems):
            copy.wait()

    return call(
        body,
        1,
        table,
        [theirs, result],
        [fixed(HALF, GCOLS), pl.BlockSpec(memory_space=pl.ANY)],
        f32(HALF, ABT * TB),
        pl.BlockSpec(memory_space=pl.ANY),
        "place",
        SMALL_MIB,
        input_output_aliases={2: 0},
        scratch_shapes=[pltpu.SemaphoreType.DMA((SIDE,))],
    )


def per_device(amplitudes, integral_tiles, integral_blocks):
    row, col = lax.axis_index("row"), lax.axis_index("col")
    z, core = row // 2, row % 2
    y, x = col // SIDE, col % SIDE
    a1 = jnp.where(core == 0, x, y)
    a2 = jnp.where(core == 0, y, x)
    wrap = lambda v: lax.rem(v + 2 * SIDE, SIDE)
    block = lambda k, h: 2 * wrap(z + k) + h

    tiles = integral_tiles.reshape(N_ROW, N_COL, TB, TB)
    coords = integral_blocks.reshape(N_ROW, N_COL, 2)[:, :, 0]
    own_rows = jnp.stack([coords[2 * wrap(z - k) + core] for k in range(SIDE)], axis=1)

    dest = lambda s, t: col_of(core, wrap(a1 + s), wrap(a2 + t))
    parts = {
        "rows": [2 * wrap(z - k) + (core + p) % 2 for p in range(2) for k in range(SIDE)],
        "near": [dest(s, 0) for s in range(SIDE)],
        "far1": [dest(s, 1) for s in range(1, SIDE)],
        "far32": [dest(s, t) for t in (3, 2) for s in range(1, SIDE)],
        "away": [block(2, 0), block(2, 1)],
        "next": [block(1, 0), block(1, 1), block(3, 0), block(3, 1)],
        "here": [block(0, 1 - core), block(0, core)],
    }
    for t in range(SIDE):
        parts[f"own{t}"] = [dest(0, t)]
        for c, name in ((core, "mine"), (1 - core, "theirs")):
            b1, b2 = jnp.where(c == 0, x, y), jnp.where(c == 0, y, x)
            parts[f"{name}{t}"] = [
                N_COL * c + col_of(c, wrap(b1 - s), wrap(b2 - t)) for s in range(SIDE)
            ]
    at, length = {}, 0
    for name, values in parts.items():
        at[name], length = length, length + len(values)
    at["places"], at["live"] = length, length + N_COL * SIDE
    table = jnp.concatenate(
        [
            jnp.stack([v for values in parts.values() for v in values]).astype(jnp.int32),
            jnp.where(own_rows >= 0, own_rows % CD_ROW, 0).astype(jnp.int32).reshape(-1),
            (own_rows >= 0).astype(jnp.int32).reshape(-1),
        ]
    )

    first = lambda arrays: [
        lax.ppermute(a, ANYWHERE, plane_shift(True, s)) for s, a in enumerate(arrays, 1)
    ]
    second = lambda array, t: lax.ppermute(array, ANYWHERE, plane_shift(False, t))
    up_z = lambda v: lax.ppermute(v, "row", z_shift(1))
    down_z = lambda v: lax.ppermute(v, "row", z_shift(-1))

    panels = [amplitudes] + [
        lax.ppermute(amplitudes, "row", z_shift(k)) for k in (1, 2, 3)
    ]
    near = pick_tiles(tiles, table, at["near"], at["rows"], 4)
    group0 = [near[0]] + first(near[1:])
    chosen = choose(panels, after(table, group0), at["places"], at["live"])
    own = lax.all_to_all(chosen, "col", split_axis=0, concat_axis=0, tiled=True)
    own = own.reshape(-1, SIDE * TB)
    amps = [own, lax.ppermute(own, "row", OTHER_CORE)]

    join = lambda t, passed, *deps: join_tiles(
        tiles, after(table, *deps), at[f"own{t}"], at["rows"], passed
    )

    def away(weights, *deps):
        half_up, half_down, *terms = products_away(after(table, *deps), at["away"], amps, weights)
        return (terms, up_z(half_up), down_z(half_down)), half_up

    def onward(state, *deps):
        terms = state[0]
        up, down = products_next(after(table, *deps), at["next"], amps, *state)
        return (terms, up_z(up), down_z(down)), up

    def here(state, t, result, before, *deps):
        theirs, result = products_here(
            after(table, *deps), at["here"], amps, *state, at[f"mine{t}"], result, before
        )
        return result, (lax.ppermute(theirs, "row", OTHER_CORE), at[f"theirs{t}"])

    far1 = pick_tiles(tiles, after(table, own), at["far1"], at["rows"], 3)
    passed1 = first(far1)
    g0, sent = away(group0, far1)
    far32 = pick_tiles(tiles, after(table, sent), at["far32"], at["rows"], 6)
    joined1 = join(1, passed1, far32)
    moved1 = second(joined1, 1)
    passed3 = first(after(far32[:3], passed1))
    g0, sent = onward(g0, joined1)
    joined3 = join(3, passed3, sent)
    moved3 = second(joined3, 3)
    passed2 = first(after(far32[3:], passed3))
    g1, sent = away([moved1], joined3)
    result, before = here(g0, 0, None, None, sent)
    g1, sent = onward(g1, result)
    joined2 = join(2, passed2, sent)
    moved2 = second(joined2, 2)
    g3, sent = away([moved3], joined2)
    g2, sent = away([moved2], sent)
    result, before = here(g1, 1, result, before, sent)
    g3, sent = onward(g3, result)
    g2, sent = onward(g2, sent)
    result, before = here(g3, 3, result, before, sent)
    result, before = here(g2, 2, result, before)
    return place(table, *before, result)


def solution(mesh):
    placed = (
        P("col", "row"),
        P(None, ("row", "col"), None, None, None),
        P(None, ("row", "col"), None, None),
    )
    return jax.shard_map(
        per_device, mesh=mesh, in_specs=placed, out_specs=P("row", "col"), check_vma=False
    )
```

time: 438 us -> 336 us (0.77)
  waiting for transfers between devices: 310 us -> 84.7 us
  Pallas kernels: 0 us -> 120 us
  matrix products: 59.5 us -> 0 us
  starting transfers between devices: 6.77 us -> 56.8 us
  blocking collectives: 19.1 us -> 53.6 us
  between operations: 13.4 us -> 0.75 us
  local copies, waits for them, and re-layouts: 27.1 us -> 16.4 us
    reduce_scatter x1 -> x0, waiting for transfers between devices: 171 us -> none  [per_device(): lax.psum_scatter(product.reshape(lax.axis_size('row') * (all_pairs // lax...]
    all_to_all x1 -> x0, waiting for transfers between devices: 139 us -> none  [per_device(): lax.all_to_all(integral_tiles, ('row', 'col'), split_axis=0, concat_axis=...]
    pallas_call x0 -> x20, Pallas kernels: none -> 120 us  [call(): pl.pallas_call(body, out_shape=out_shape, grid_spec=pltpu.PrefetchScalarG...]
    ppermute x0 -> x39, waiting for transfers between devices: none -> 84.7 us  [the longest x8 28.9 us: per_device(): down_z = lambda v: lax.ppermute(v, 'row', z_shift(-1))]
    dot_general x1 -> x0, matrix products: 59.5 us -> none  [per_device(): jnp.einsum('pqx,qaxy->pay', chosen, tile_groups, precision=lax.Precision....]
    ppermute x0 -> x39, starting transfers between devices: none -> 56.8 us  [the longest x8 17.6 us: per_device(): down_z = lambda v: lax.ppermute(v, 'row', z_shift(-1))]
    all_to_all x1, blocking collectives: 19.1 us -> 53.6 us  [per_device(): own = lax.all_to_all(chosen, 'col', split_axis=0, concat_axis=0, tiled=True)]
    reshape x2 -> x1, local copies, waits for them, and re-layouts: 18.1 us -> 0.75 us  [per_device(): coords = integral_blocks.reshape(N_ROW, N_COL, 2)[:, :, 0]]
  transfers between devices with their start and end apart: 3 -> 39, of which waited for: 2 -> 17; matrix products, arithmetic and copies ran while one was open for 2% -> 0% of each run, Pallas kernels for 0% -> 30%
where the time goes in v1:
time: 336 us; the launch traced here: 333 us
  Pallas kernels  120 us (36%)
  waiting for transfers between devices  84.7 us (25%)
  starting transfers between devices  56.8 us (17%)
  blocking collectives  53.6 us (16%)
  local copies, waits for them, and re-layouts  16.4 us (5%)
    pallas_call x20, Pallas kernels, call(): pl.pallas_call(body, out_shape=out_shape, grid_spec=pltpu.PrefetchScalarG...  120 us
    all_to_all x1, blocking collectives, per_device(): own = lax.all_to_all(chosen, 'col', split_axis=0, concat_axis=0, tiled=True)  53.6 us
    ppermute x8, waiting for transfers between devices, per_device(): down_z = lambda v: lax.ppermute(v, 'row', z_shift(-1))  28.9 us
    ppermute x8, starting transfers between devices, per_device(): down_z = lambda v: lax.ppermute(v, 'row', z_shift(-1))  17.6 us
    ppermute x3, waiting for transfers between devices, per_device(): lax.ppermute(amplitudes, 'row', z_shift(k))  15.6 us
    ppermute x3, waiting for transfers between devices, per_device(): lax.ppermute(array, ANYWHERE, plane_shift(False, t))  15.1 us
    ppermute x12, starting transfers between devices, per_device(): lax.ppermute(a, ANYWHERE, plane_shift(True, s))  14.9 us
    unnamed x94, local copies, waits for them, and re-layouts  14.7 us
  transfers between devices with their start and end apart: 39, of which 17 were waited for; matrix products, arithmetic and copies ran while one was open for 0% of the time, Pallas kernels for 30%

profile of v1, /device:TPU:3, one launch (start us, length us, event | category | flops | bytes accessed | tf_op | source)
XLA Modules:
  0.0 332.7 jit_solution(42299559395366382)
XLA Ops:
  1.9 4.5 %pick_tiles.3 = (f32[1,8,128,128]{3,2,1,0:T(8,128)}, f32[1,8,128,128]{3,2,1,0:T(8,128)}, f32[1,8,128,128]{3,2,1,0:T(8,128)}, f32[1,8,128,128]{3,2,1,0:T(8,128)}) custom-call(s32[193]{0:T(256)} %concatenate.3.table_ref, f32[8,16,128,128]{3,2,1,0:T(8,128)} %bitcast.98), custom_call_target="tpu_custom_call" | custom-call | bytes 1024 | tf_op jit(solution)/shard_map/pick_tiles/pallas_call | solution.py:60
  6.4 1.3 collective-permute-start
  7.7 2.6 collective-permute-start.1
  10.4 1.1 collective-permute-start.2
  11.4 3.6 %collective-permute-start.4 = (f32[128,1024]{1,0:T(8,128)S(1)}, f32[128,1024]{1,0:T(8,128)S(1)}, u32[]{:S(2)}, u32[]{:S(2)}) collective-permute-start(f32[128,1024]{1,0:T(8,128)S(1)} %copy-done), channel_id=1, source_target_pairs={{0,64},{16,80},{32,96},{48,112},{64,0},{80,16},{96,32},{112,48},{1... | collective-permute-start | bytes 1572872 | tf_op jit(solution)/shard_map/ppermute | solution.py:397
  16.1 3.8 %collective-permute-start.5 = (f32[128,1024]{1,0:T(8,128)S(1)}, f32[128,1024]{1,0:T(8,128)S(1)}, u32[]{:S(2)}, u32[]{:S(2)}) collective-permute-start(f32[128,1024]{1,0:T(8,128)S(1)} %copy-done), channel_id=1, source_target_pairs={{0,96},{16,112},{32,0},{48,16},{64,32},{80,48},{96,64},{112,80},{1... | collective-permute-start | bytes 1572872 | tf_op jit(solution)/shard_map/ppermute | solution.py:397
  19.8 3.2 collective-permute-done.1.refs_4_
  23.0 3.9 %collective-permute-done.4.refs_2_ = f32[128,1024]{1,0:T(8,128)S(1)} collective-permute-done((f32[128,1024]{1,0:T(8,128)S(1)}, f32[128,1024]{1,0:T(8,128)S(1)}, u32[]{:S(2)}, u32[]{:S(2)}) %collective-permute-start.4) | collective-permute-done | bytes 524320 | tf_op jit(solution)/shard_map/ppermute | solution.py:397
  27.0 11.7 %collective-permute-done.3.refs_1_ = f32[128,1024]{1,0:T(8,128)S(1)} collective-permute-done((f32[128,1024]{1,0:T(8,128)S(1)}, f32[128,1024]{1,0:T(8,128)S(1)}, u32[]{:S(2)}, u32[]{:S(2)}) %collective-permute-start.3) | collective-permute-done | bytes 524320 | tf_op jit(solution)/shard_map/ppermute | solution.py:397
  38.6 1.4 choose.1
  40.0 53.6 %all_to_all.5 = f32[16,128,512]{2,1,0:T(8,128)S(1)} all-to-all(f32[16,128,512]{2,1,0:T(8,128)S(1)} %choose.1), channel_id=1, replica_groups=mesh['row'=8,'col'=16] {'col'}, dimensions={0} | all-to-all | bytes 8388608 | tf_op jit(solution)/shard_map/all_to_all | solution.py:402
  93.6 2.1 collective-permute-start.6
  95.7 4.0 %pick_tiles.4 = (f32[1,8,128,128]{3,2,1,0:T(8,128)}, f32[1,8,128,128]{3,2,1,0:T(8,128)}, f32[1,8,128,128]{3,2,1,0:T(8,128)}) custom-call(s32[193]{0:T(256)} %concatenate.3.table_ref, f32[8,16,128,128]{3,2,1,0:T(8,128)} %bitcast.99), custom_call_target="tpu_custom_call" | custom-call | bytes 1024 | tf_op jit(solution)/shard_map/pick_tiles/pallas_call | solution.py:60
  99.8 1.8 collective-permute-start.8
  101.5 0.9 collective-permute-start.9
  102.7 6.8 %products_away.4 = (f32[256,512]{1,0:T(8,128)}, f32[256,512]{1,0:T(8,128)}, bf16[1024,512]{1,0:T(8,128)(2,1)}, bf16[1024,512]{1,0:T(8,128)(2,1)}) custom-call(s32[193]{0:T(256)} %concatenate.3.table_ref, f32[2048,512]{1,0:T(8,128)} %bitcast.86, f32[2048,512]{1,0:T(8,128)} %collective-permute-done.6.refs_1_, f32[1,8,128,128]{3,2,1,0:T(8,128)} %get-tuple-element.73.refs_2_, ...), custom_call_target="tpu_custom_call" | custom-call | bytes 1024 | tf_op jit(solution)/shard_map/products_away/pallas_call | solution.py:60
  109.5 5.9 %pick_tiles.5 = (f32[1,8,128,128]{3,2,1,0:T(8,128)}, f32[1,8,128,128]{3,2,1,0:T(8,128)}, f32[1,8,128,128]{3,2,1,0:T(8,128)}, f32[1,8,128,128]{3,2,1,0:T(8,128)},...) custom-call(s32[193]{0:T(256)} %concatenate.3.table_ref, f32[8,16,128,128]{3,2,1,0:T(8,128)} %bitcast.100), custom_call_target="tpu_custom_call" | custom-call | bytes 1024 | tf_op jit(solution)/shard_map/pick_tiles/pallas_call | solution.py:60
  117.2 4.1 %join_tiles.3 = f32[4,8,128,128]{3,2,1,0:T(8,128)} custom-call(s32[193]{0:T(256)} %concatenate.3.table_ref, f32[8,16,128,128]{3,2,1,0:T(8,128)} %bitcast.101, f32[1,8,128,128]{3,2,1,0:T(8,128)} %copy-done.25, f32[1,8,128,128]{3,2,1,0:T(8,128)} %copy-done.28, f32[1,8,128,128]{3,2,1,0:T(8,128)} %copy-done.29), custom_call_target="tpu_custom_call" | custom-call | bytes 1024 | tf_op jit(solution)/shard_map/join_tiles/pallas_call | solution.py:60
  121.6 2.4 collective-permute-start.11
  124.3 9.9 %collective-permute-done.11.refs_5_ = f32[256,512]{1,0:T(8,128)S(1)} collective-permute-done((f32[256,512]{1,0:T(8,128)S(1)}, f32[256,512]{1,0:T(8,128)S(1)}, u32[]{:S(2)}, u32[]{:S(2)}) %collective-permute-start.11) | collective-permute-done | bytes 524320 | tf_op jit(solution)/shard_map/ppermute | solution.py:394
  134.2 3.1 collective-permute-done.10.refs_4_
  138.1 8.6 %products_next.4 = (f32[512,512]{1,0:T(8,128)}, f32[512,512]{1,0:T(8,128)}) custom-call(s32[193]{0:T(256)} %concatenate.3.table_ref, f32[2048,512]{1,0:T(8,128)} %bitcast.87, f32[2048,512]{1,0:T(8,128)} %collective-permute-done.6.refs_1_, bf16[1024,512]{1,0:T(8,128)(2,1)} %get-tuple-element.93.refs_2_, bf16[1024,512]{1,0:T(8,128)(2,1)} %get-tuple-element.94.refs_3_, ...), custom_call_target="tpu_custom_call" | custom-call | bytes 1024 | tf_op jit(solution)/shard_map/products_next/pallas_call | solution.py:60
  147.2 1.0 collective-permute-start.16
  148.2 1.8 collective-permute-start.13
  150.4 9.4 %collective-permute-done.13.refs_1_ = f32[1,8,128,128]{3,2,1,0:T(8,128)S(1)} collective-permute-done((f32[1,8,128,128]{3,2,1,0:T(8,128)S(1)}, f32[1,8,128,128]{3,2,1,0:T(8,128)S(1)}, u32[]{:S(2)}, u32[]{:S(2)}) %collective-permute-start.13) | collective-permute-done | bytes 524320 | tf_op jit(solution)/shard_map/ppermute | solution.py:390
  159.9 0.8 collective-permute-done.14.refs_2_
  161.5 4.1 %join_tiles.4 = f32[4,8,128,128]{3,2,1,0:T(8,128)} custom-call(s32[193]{0:T(256)} %concatenate.3.table_ref, f32[8,16,128,128]{3,2,1,0:T(8,128)} %bitcast.102, f32[1,8,128,128]{3,2,1,0:T(8,128)} %copy-done.22, f32[1,8,128,128]{3,2,1,0:T(8,128)} %copy-done.32, f32[1,8,128,128]{3,2,1,0:T(8,128)} %copy-done.34), custom_call_target="tpu_custom_call" | custom-call | bytes 1024 | tf_op jit(solution)/shard_map/join_tiles/pallas_call | solution.py:60
  165.6 1.3 copy-done.5
  166.9 6.8 %products_away.5 = (f32[256,512]{1,0:T(8,128)}, f32[256,512]{1,0:T(8,128)}, bf16[1024,512]{1,0:T(8,128)(2,1)}, bf16[1024,512]{1,0:T(8,128)(2,1)}) custom-call(s32[193]{0:T(256)} %concatenate.3.table_ref, f32[2048,512]{1,0:T(8,128)} %bitcast.88, f32[2048,512]{1,0:T(8,128)} %collective-permute-done.6.refs_1_, f32[4,8,128,128]{3,2,1,0:T(8,128)} %copy-done.5), custom_call_target="tpu_custom_call" | custom-call | bytes 1024 | tf_op jit(solution)/shard_map/products_away/pallas_call | solution.py:60
  173.7 2.4 collective-permute-start.19
  176.1 1.9 collective-permute-start.20
  178.0 1.1 collective-permute-start.21
  179.1 1.8 collective-permute-start.22
  180.8 6.8 %products_here.4 = (f32[256,512]{1,0:T(8,128)}, f32[256,4096]{1,0:T(8,128)}) custom-call(s32[193]{0:T(256)} %concatenate.3.table_ref, f32[2048,512]{1,0:T(8,128)} %bitcast.89, f32[2048,512]{1,0:T(8,128)} %collective-permute-done.6.refs_1_, bf16[1024,512]{1,0:T(8,128)(2,1)} %get-tuple-element.93.refs_2_, bf16[1024,512]{1,0:T(8,128)(2,1)} %get-tuple-element.94.refs_3_, ...), custom_call_target="tpu_custom_call" | custom-call | bytes 1024 | tf_op jit(solution)/shard_map/products_here/pallas_call | solution.py:60
  187.7 1.5 collective-permute-start.23
  189.2 0.8 copy-done.23
  190.0 8.4 %products_next.5 = (f32[512,512]{1,0:T(8,128)}, f32[512,512]{1,0:T(8,128)}) custom-call(s32[193]{0:T(256)} %concatenate.3.table_ref, f32[2048,512]{1,0:T(8,128)} %bitcast.90, f32[2048,512]{1,0:T(8,128)} %collective-permute-done.6.refs_1_, bf16[1024,512]{1,0:T(8,128)(2,1)} %get-tuple-element.107.refs_2_, bf16[1024,512]{1,0:T(8,128)(2,1)} %get-tuple-element.108.refs_3_, ...), custom_call_target="tpu_custom_call" | custom-call | bytes 1024 | tf_op jit(solution)/shard_map/products_next/pallas_call | solution.py:60
  200.2 4.1 %join_tiles.5 = f32[4,8,128,128]{3,2,1,0:T(8,128)} custom-call(s32[193]{0:T(256)} %concatenate.3.table_ref, f32[8,16,128,128]{3,2,1,0:T(8,128)} %bitcast.103, f32[1,8,128,128]{3,2,1,0:T(8,128)} %copy-done.17, f32[1,8,128,128]{3,2,1,0:T(8,128)} %copy-done.21, f32[1,8,128,128]{3,2,1,0:T(8,128)} %copy-done.27), custom_call_target="tpu_custom_call" | custom-call | bytes 1024 | tf_op jit(solution)/shard_map/join_tiles/pallas_call | solution.py:60
  204.3 2.4 collective-permute-start.24
  206.7 2.7 collective-permute-start.26
  209.4 8.5 %collective-permute-start.27 = (f32[256,512]{1,0:T(8,128)}, f32[256,512]{1,0:T(8,128)S(1)}, u32[]{:S(2)}, u32[]{:S(2)}) collective-permute-start(f32[256,512]{1,0:T(8,128)} %get-tuple-element.123), channel_id=1, source_target_pairs={{0,16},{16,0},{32,48},{48,32},{64,80},{80,64},{96,112},{112,96},{1... | collective-permute-start | bytes 1572872 | tf_op jit(solution)/shard_map/ppermute | solution.py:423
  217.9 3.6 %collective-permute-done.23.refs_2_ = f32[4,8,128,128]{3,2,1,0:T(8,128)S(1)} collective-permute-done((f32[4,8,128,128]{3,2,1,0:T(8,128)S(1)}, f32[4,8,128,128]{3,2,1,0:T(8,128)S(1)}, u32[]{:S(2)}, u32[]{:S(2)}) %collective-permute-start.23) | collective-permute-done | bytes 2097184 | tf_op jit(solution)/shard_map/ppermute | solution.py:392
  221.4 1.4 copy-done.6
  222.8 6.8 %products_away.6 = (f32[256,512]{1,0:T(8,128)}, f32[256,512]{1,0:T(8,128)}, bf16[1024,512]{1,0:T(8,128)(2,1)}, bf16[1024,512]{1,0:T(8,128)(2,1)}) custom-call(s32[193]{0:T(256)} %concatenate.3.table_ref, f32[2048,512]{1,0:T(8,128)} %bitcast.91, f32[2048,512]{1,0:T(8,128)} %collective-permute-done.6.refs_1_, f32[4,8,128,128]{3,2,1,0:T(8,128)} %copy-done.6), custom_call_target="tpu_custom_call" | custom-call | bytes 1024 | tf_op jit(solution)/shard_map/products_away/pallas_call | solution.py:60
  229.6 2.8 collective-permute-start.29
  232.4 11.6 %collective-permute-done.24.refs_2_ = f32[4,8,128,128]{3,2,1,0:T(8,128)S(1)} collective-permute-done((f32[4,8,128,128]{3,2,1,0:T(8,128)}, f32[4,8,128,128]{3,2,1,0:T(8,128)S(1)}, u32[]{:S(2)}, u32[]{:S(2)}) %collective-permute-start.24) | collective-permute-done | bytes 2097184 | tf_op jit(solution)/shard_map/ppermute | solution.py:392
  244.0 1.3 copy-done.7
  245.3 6.9 %products_away.7 = (f32[256,512]{1,0:T(8,128)}, f32[256,512]{1,0:T(8,128)}, bf16[1024,512]{1,0:T(8,128)(2,1)}, bf16[1024,512]{1,0:T(8,128)(2,1)}) custom-call(s32[193]{0:T(256)} %concatenate.3.table_ref, f32[2048,512]{1,0:T(8,128)} %bitcast.92, f32[2048,512]{1,0:T(8,128)} %collective-permute-done.6.refs_1_, f32[4,8,128,128]{3,2,1,0:T(8,128)} %copy-done.7), custom_call_target="tpu_custom_call" | custom-call | bytes 1024 | tf_op jit(solution)/shard_map/products_away/pallas_call | solution.py:60
  253.4 7.6 %products_here.5 = (f32[256,512]{1,0:T(8,128)}, f32[256,4096]{1,0:T(8,128)}) custom-call(s32[193]{0:T(256)} %concatenate.3.table_ref, f32[2048,512]{1,0:T(8,128)} %bitcast.93, f32[2048,512]{1,0:T(8,128)} %collective-permute-done.6.refs_1_, bf16[1024,512]{1,0:T(8,128)(2,1)} %get-tuple-element.107.refs_2_, ...), custom_call_target="tpu_custom_call", output_to_operand_aliasing={{1}: (8, {})} | custom-call | bytes 1024 | tf_op jit(solution)/shard_map/products_here/pallas_call | solution.py:60
  260.9 2.9 collective-permute-start.31
  264.9 8.5 %products_next.6 = (f32[512,512]{1,0:T(8,128)}, f32[512,512]{1,0:T(8,128)}) custom-call(s32[193]{0:T(256)} %concatenate.3.table_ref, f32[2048,512]{1,0:T(8,128)} %bitcast.94, f32[2048,512]{1,0:T(8,128)} %collective-permute-done.6.refs_1_, bf16[1024,512]{1,0:T(8,128)(2,1)} %get-tuple-element.126.refs_2_, bf16[1024,512]{1,0:T(8,128)(2,1)} %get-tuple-element.127.refs_3_, ...), custom_call_target="tpu_custom_call" | custom-call | bytes 1024 | tf_op jit(solution)/shard_map/products_next/pallas_call | solution.py:60
  273.4 1.4 collective-permute-start.35
  275.9 8.4 %products_next.7 = (f32[512,512]{1,0:T(8,128)}, f32[512,512]{1,0:T(8,128)}) custom-call(s32[193]{0:T(256)} %concatenate.3.table_ref, f32[2048,512]{1,0:T(8,128)} %bitcast.95, f32[2048,512]{1,0:T(8,128)} %collective-permute-done.6.refs_1_, bf16[1024,512]{1,0:T(8,128)(2,1)} %get-tuple-element.118.refs_2_, bf16[1024,512]{1,0:T(8,128)(2,1)} %get-tuple-element.119.refs_3_, ...), custom_call_target="tpu_custom_call" | custom-call | bytes 1024 | tf_op jit(solution)/shard_map/products_next/pallas_call | solution.py:60
  284.3 2.6 collective-permute-start.33
  286.9 12.0 %collective-permute-done.35.refs_5_ = f32[512,512]{1,0:T(8,128)S(1)} collective-permute-done((f32[512,512]{1,0:T(8,128)}, f32[512,512]{1,0:T(8,128)S(1)}, u32[]{:S(2)}, u32[]{:S(2)}) %collective-permute-start.35) | collective-permute-done | bytes 1048608 | tf_op jit(solution)/shard_map/ppermute | solution.py:394
  298.9 2.6 collective-permute-done.34.refs_4_
  301.4 1.0 copy-done.13
  302.4 7.6 %products_here.6 = (f32[256,512]{1,0:T(8,128)}, f32[256,4096]{1,0:T(8,128)}) custom-call(s32[193]{0:T(256)} %concatenate.3.table_ref, f32[2048,512]{1,0:T(8,128)} %bitcast.96, f32[2048,512]{1,0:T(8,128)} %collective-permute-done.6.refs_1_, bf16[1024,512]{1,0:T(8,128)(2,1)} %get-tuple-element.126.refs_2_, ...), custom_call_target="tpu_custom_call", output_to_operand_aliasing={{1}: (8, {})} | custom-call | bytes 1024 | tf_op jit(solution)/shard_map/products_here/pallas_call | solution.py:60
  310.1 7.1 %collective-permute-done.33.refs_5_ = f32[512,512]{1,0:T(8,128)S(1)} collective-permute-done((f32[512,512]{1,0:T(8,128)}, f32[512,512]{1,0:T(8,128)S(1)}, u32[]{:S(2)}, u32[]{:S(2)}) %collective-permute-start.33) | collective-permute-done | bytes 1048608 | tf_op jit(solution)/shard_map/ppermute | solution.py:394
  317.2 2.9 collective-permute-done.32.refs_4_
  320.1 1.0 copy-done.14
  321.2 7.7 %products_here.7 = (f32[256,512]{1,0:T(8,128)}, f32[256,4096]{1,0:T(8,128)}) custom-call(s32[193]{0:T(256)} %concatenate.3.table_ref, f32[2048,512]{1,0:T(8,128)} %bitcast.97, f32[2048,512]{1,0:T(8,128)} %collective-permute-done.6.refs_1_, bf16[1024,512]{1,0:T(8,128)(2,1)} %get-tuple-element.118.refs_2_, ...), custom_call_target="tpu_custom_call", output_to_operand_aliasing={{1}: (8, {})} | custom-call | bytes 1024 | tf_op jit(solution)/shard_map/products_here/pallas_call | solution.py:60
  329.0 2.1 collective-permute-done.38.theirs_ref
  331.1 1.4 place.1
  (138 shorter events, 13.2 us)
Async XLA Ops:
  1.9 9.5 %copy-start = (f32[128,1024]{1,0:T(8,128)S(1)}, f32[128,1024]{1,0:T(8,128)}, u32[]{:S(2)}) copy-start(f32[128,1024]{1,0:T(8,128)} %refs_0_.1) | copy-start | bytes 1572868
  1.9 36.7 %copy-start.1 = (s32[193]{0:T(256)S(1)}, s32[193]{0:T(256)}, u32[]{:S(2)}) copy-start(s32[193]{0:T(256)} %concatenate.3.table_ref) | copy-start | bytes 2320
  6.4 9.7 %collective-permute-start = (f32[1,8,128,128]{3,2,1,0:T(8,128)}, f32[1,8,128,128]{3,2,1,0:T(8,128)S(1)}, u32[]{:S(2)}, u32[]{:S(2)}) collective-permute-start(f32[1,8,128,128]{3,2,1,0:T(8,128)} %get-tuple-element.74), channel_id=1, source_target_pairs={{0,1},{1,2},{2,3},{3,0},{4,5},{5,6},{6,7},{7,4},{8,9},{9,10},{10,1... | collective-permute-start | bytes 1572872 | tf_op jit(solution)/shard_map/ppermute | solution.py:390
  7.7 15.3 %collective-permute-start.1 = (f32[1,8,128,128]{3,2,1,0:T(8,128)}, f32[1,8,128,128]{3,2,1,0:T(8,128)S(1)}, u32[]{:S(2)}, u32[]{:S(2)}) collective-permute-start(f32[1,8,128,128]{3,2,1,0:T(8,128)} %get-tuple-element.75), channel_id=1, source_target_pairs={{0,2},{1,3},{2,0},{3,1},{4,6},{5,7},{6,4},{7,5},{8,10},{9,11},{10,... | collective-permute-start | bytes 1572872 | tf_op jit(solution)/shard_map/ppermute | solution.py:390
  10.4 12.7 %collective-permute-start.2 = (f32[1,8,128,128]{3,2,1,0:T(8,128)}, f32[1,8,128,128]{3,2,1,0:T(8,128)S(1)}, u32[]{:S(2)}, u32[]{:S(2)}) collective-permute-start(f32[1,8,128,128]{3,2,1,0:T(8,128)} %get-tuple-element.76), channel_id=1, source_target_pairs={{0,3},{1,0},{2,1},{3,2},{4,7},{5,4},{6,5},{7,6},{8,11},{9,8},{10,9... | collective-permute-start | bytes 1572872 | tf_op jit(solution)/shard_map/ppermute | solution.py:390
  11.4 15.5 %collective-permute-start.4 = (f32[128,1024]{1,0:T(8,128)S(1)}, f32[128,1024]{1,0:T(8,128)S(1)}, u32[]{:S(2)}, u32[]{:S(2)}) collective-permute-start(f32[128,1024]{1,0:T(8,128)S(1)} %copy-done), channel_id=1, source_target_pairs={{0,64},{16,80},{32,96},{48,112},{64,0},{80,16},{96,32},{112,48},{1... | collective-permute-start | bytes 1572872 | tf_op jit(solution)/shard_map/ppermute | solution.py:397
  15.0 23.6 %collective-permute-start.3 = (f32[128,1024]{1,0:T(8,128)S(1)}, f32[128,1024]{1,0:T(8,128)S(1)}, u32[]{:S(2)}, u32[]{:S(2)}) collective-permute-start(f32[128,1024]{1,0:T(8,128)S(1)} %copy-done), channel_id=1, source_target_pairs={{0,32},{16,48},{32,64},{48,80},{64,96},{80,112},{96,0},{112,16},{1... | collective-permute-start | bytes 1572872 | tf_op jit(solution)/shard_map/ppermute | solution.py:397
  16.1 77.5 %copy-start.35 = (f32[1,8,128,128]{3,2,1,0:T(8,128)}, f32[1,8,128,128]{3,2,1,0:T(8,128)S(1)}, u32[]{:S(2)}) copy-start(f32[1,8,128,128]{3,2,1,0:T(8,128)S(1)} %collective-permute-done.refs_3_) | copy-start | bytes 1572868
  16.1 22.6 %collective-permute-start.5 = (f32[128,1024]{1,0:T(8,128)S(1)}, f32[128,1024]{1,0:T(8,128)S(1)}, u32[]{:S(2)}, u32[]{:S(2)}) collective-permute-start(f32[128,1024]{1,0:T(8,128)S(1)} %copy-done), channel_id=1, source_target_pairs={{0,96},{16,112},{32,0},{48,16},{64,32},{80,48},{96,64},{112,80},{1... | collective-permute-start | bytes 1572872 | tf_op jit(solution)/shard_map/ppermute | solution.py:397
  23.0 70.6 %copy-start.36 = (f32[1,8,128,128]{3,2,1,0:T(8,128)}, f32[1,8,128,128]{3,2,1,0:T(8,128)S(1)}, u32[]{:S(2)}) copy-start(f32[1,8,128,128]{3,2,1,0:T(8,128)S(1)} %collective-permute-done.1.refs_4_) | copy-start | bytes 1572868
  23.0 70.6 %copy-start.37 = (f32[1,8,128,128]{3,2,1,0:T(8,128)}, f32[1,8,128,128]{3,2,1,0:T(8,128)S(1)}, u32[]{:S(2)}) copy-start(f32[1,8,128,128]{3,2,1,0:T(8,128)S(1)} %collective-permute-done.2.refs_5_) | copy-start | bytes 1572868
  93.6 6.2 %copy-start.3 = (f32[16,128,512]{2,1,0:T(8,128)}, f32[16,128,512]{2,1,0:T(8,128)S(1)}, u32[]{:S(2)}) copy-start(f32[16,128,512]{2,1,0:T(8,128)S(1)} %all_to_all.5) | copy-start | bytes 12582916
  93.6 9.0 %collective-permute-start.6 = (f32[2048,512]{1,0:T(8,128)S(1)}, f32[2048,512]{1,0:T(8,128)}, u32[]{:S(2)}, u32[]{:S(2)}) collective-permute-start(f32[2048,512]{1,0:T(8,128)S(1)} %bitcast.85), channel_id=1, source_target_pairs={{0,16},{16,0},{32,48},{48,32},{64,80},{80,64},{96,112},{112,96},{1... | collective-permute-start | bytes 12582920 | tf_op jit(solution)/shard_map/ppermute | solution.py:404
  99.8 15.6 %collective-permute-start.7 = (f32[1,8,128,128]{3,2,1,0:T(8,128)}, f32[1,8,128,128]{3,2,1,0:T(8,128)S(1)}, u32[]{:S(2)}, u32[]{:S(2)}) collective-permute-start(f32[1,8,128,128]{3,2,1,0:T(8,128)} %get-tuple-element.79), channel_id=1, source_target_pairs={{0,1},{1,2},{2,3},{3,0},{4,5},{5,6},{6,7},{7,4},{8,9},{9,10},{10,1... | collective-permute-start | bytes 1572872 | tf_op jit(solution)/shard_map/ppermute | solution.py:390
  99.8 15.6 %collective-permute-start.8 = (f32[1,8,128,128]{3,2,1,0:T(8,128)}, f32[1,8,128,128]{3,2,1,0:T(8,128)S(1)}, u32[]{:S(2)}, u32[]{:S(2)}) collective-permute-start(f32[1,8,128,128]{3,2,1,0:T(8,128)} %get-tuple-element.80), channel_id=1, source_target_pairs={{0,2},{1,3},{2,0},{3,1},{4,6},{5,7},{6,4},{7,5},{8,10},{9,11},{10,... | collective-permute-start | bytes 1572872 | tf_op jit(solution)/shard_map/ppermute | solution.py:390
  101.5 14.2 %collective-permute-start.9 = (f32[1,8,128,128]{3,2,1,0:T(8,128)}, f32[1,8,128,128]{3,2,1,0:T(8,128)S(1)}, u32[]{:S(2)}, u32[]{:S(2)}) collective-permute-start(f32[1,8,128,128]{3,2,1,0:T(8,128)} %get-tuple-element.81), channel_id=1, source_target_pairs={{0,3},{1,0},{2,1},{3,2},{4,7},{5,4},{6,5},{7,6},{8,11},{9,8},{10,9... | collective-permute-start | bytes 1572872 | tf_op jit(solution)/shard_map/ppermute | solution.py:390
  115.4 6.3 %copy-start.46 = (f32[256,512]{1,0:T(8,128)S(1)}, f32[256,512]{1,0:T(8,128)}, u32[]{:S(2)}) copy-start(f32[256,512]{1,0:T(8,128)} %get-tuple-element.95) | copy-start | bytes 1572868
  115.4 8.7 %copy-start.45 = (f32[256,512]{1,0:T(8,128)S(1)}, f32[256,512]{1,0:T(8,128)}, u32[]{:S(2)}) copy-start(f32[256,512]{1,0:T(8,128)} %get-tuple-element.83) | copy-start | bytes 1572868
  115.4 8.7 %copy-start.42 = (f32[1,8,128,128]{3,2,1,0:T(8,128)S(1)}, f32[1,8,128,128]{3,2,1,0:T(8,128)}, u32[]{:S(2)}) copy-start(f32[1,8,128,128]{3,2,1,0:T(8,128)} %get-tuple-element.98) | copy-start | bytes 1572868
  121.3 44.3 %collective-permute-start.15 = (f32[4,8,128,128]{3,2,1,0:T(8,128)}, f32[4,8,128,128]{3,2,1,0:T(8,128)S(1)}, u32[]{:S(2)}, u32[]{:S(2)}) collective-permute-start(f32[4,8,128,128]{3,2,1,0:T(8,128)} %join_tiles.3), channel_id=1, source_target_pairs={{0,4},{1,5},{2,6},{3,7},{4,8},{5,9},{6,10},{7,11},{8,12},{9,13},{1... | collective-permute-start | bytes 6291464 | tf_op jit(solution)/shard_map/ppermute | solution.py:392
  121.6 12.5 %collective-permute-start.11 = (f32[256,512]{1,0:T(8,128)S(1)}, f32[256,512]{1,0:T(8,128)S(1)}, u32[]{:S(2)}, u32[]{:S(2)}) collective-permute-start(f32[256,512]{1,0:T(8,128)S(1)} %copy-done.46), channel_id=1, source_target_pairs={{0,96},{16,112},{32,0},{48,16},{64,32},{80,48},{96,64},{112,80},{1... | collective-permute-start | bytes 1572872 | tf_op jit(solution)/shard_map/ppermute | solution.py:394
  124.1 13.2 %collective-permute-start.10 = (f32[256,512]{1,0:T(8,128)S(1)}, f32[256,512]{1,0:T(8,128)S(1)}, u32[]{:S(2)}, u32[]{:S(2)}) collective-permute-start(f32[256,512]{1,0:T(8,128)S(1)} %copy-done.45), channel_id=1, source_target_pairs={{0,32},{16,48},{32,64},{48,80},{64,96},{80,112},{96,0},{112,16},{1... | collective-permute-start | bytes 1572872 | tf_op jit(solution)/shard_map/ppermute | solution.py:393
  124.1 25.9 %collective-permute-start.12 = (f32[1,8,128,128]{3,2,1,0:T(8,128)S(1)}, f32[1,8,128,128]{3,2,1,0:T(8,128)S(1)}, u32[]{:S(2)}, u32[]{:S(2)}) collective-permute-start(f32[1,8,128,128]{3,2,1,0:T(8,128)S(1)} %copy-done.42), channel_id=1, source_target_pairs={{0,1},{1,2},{2,3},{3,0},{4,5},{5,6},{6,7},{7,4},{8,9},{9,10},{10,1... | collective-permute-start | bytes 1572872 | tf_op jit(solution)/shard_map/ppermute | solution.py:390
  134.2 3.1 copy-start.31
  138.1 10.1 %copy-start.41 = (f32[1,8,128,128]{3,2,1,0:T(8,128)S(1)}, f32[1,8,128,128]{3,2,1,0:T(8,128)}, u32[]{:S(2)}) copy-start(f32[1,8,128,128]{3,2,1,0:T(8,128)} %get-tuple-element.99) | copy-start | bytes 1572868
  138.1 11.9 %copy-start.40 = (f32[1,8,128,128]{3,2,1,0:T(8,128)S(1)}, f32[1,8,128,128]{3,2,1,0:T(8,128)}, u32[]{:S(2)}) copy-start(f32[1,8,128,128]{3,2,1,0:T(8,128)} %get-tuple-element.100) | copy-start | bytes 1572868
  146.7 31.3 %collective-permute-start.17 = (f32[512,512]{1,0:T(8,128)}, f32[512,512]{1,0:T(8,128)S(1)}, u32[]{:S(2)}, u32[]{:S(2)}) collective-permute-start(f32[512,512]{1,0:T(8,128)} %get-tuple-element.104), channel_id=1, source_target_pairs={{0,96},{16,112},{32,0},{48,16},{64,32},{80,48},{96,64},{112,80},{1... | collective-permute-start | bytes 3145736 | tf_op jit(solution)/shard_map/ppermute | solution.py:394
  147.2 31.9 %collective-permute-start.16 = (f32[512,512]{1,0:T(8,128)}, f32[512,512]{1,0:T(8,128)S(1)}, u32[]{:S(2)}, u32[]{:S(2)}) collective-permute-start(f32[512,512]{1,0:T(8,128)} %get-tuple-element.96), channel_id=1, source_target_pairs={{0,32},{16,48},{32,64},{48,80},{64,96},{80,112},{96,0},{112,16},{1... | collective-permute-start | bytes 3145736 | tf_op jit(solution)/shard_map/ppermute | solution.py:393
  148.2 11.7 %collective-permute-start.13 = (f32[1,8,128,128]{3,2,1,0:T(8,128)S(1)}, f32[1,8,128,128]{3,2,1,0:T(8,128)S(1)}, u32[]{:S(2)}, u32[]{:S(2)}) collective-permute-start(f32[1,8,128,128]{3,2,1,0:T(8,128)S(1)} %copy-done.41), channel_id=1, source_target_pairs={{0,2},{1,3},{2,0},{3,1},{4,6},{5,7},{6,4},{7,5},{8,10},{9,11},{10,... | collective-permute-start | bytes 1572872 | tf_op jit(solution)/shard_map/ppermute | solution.py:390
  150.0 10.7 %copy-start.22 = (f32[1,8,128,128]{3,2,1,0:T(8,128)}, f32[1,8,128,128]{3,2,1,0:T(8,128)S(1)}, u32[]{:S(2)}) copy-start(f32[1,8,128,128]{3,2,1,0:T(8,128)S(1)} %collective-permute-done.12.refs_0_) | copy-start | bytes 1572868
  150.0 10.7 %collective-permute-start.14 = (f32[1,8,128,128]{3,2,1,0:T(8,128)S(1)}, f32[1,8,128,128]{3,2,1,0:T(8,128)S(1)}, u32[]{:S(2)}, u32[]{:S(2)}) collective-permute-start(f32[1,8,128,128]{3,2,1,0:T(8,128)S(1)} %copy-done.40), channel_id=1, source_target_pairs={{0,3},{1,0},{2,1},{3,2},{4,7},{5,4},{6,5},{7,6},{8,11},{9,8},{10,9... | collective-permute-start | bytes 1572872 | tf_op jit(solution)/shard_map/ppermute | solution.py:390
  165.6 12.4 %copy-start.39 = (f32[1,8,128,128]{3,2,1,0:T(8,128)S(1)}, f32[1,8,128,128]{3,2,1,0:T(8,128)}, u32[]{:S(2)}) copy-start(f32[1,8,128,128]{3,2,1,0:T(8,128)} %get-tuple-element.113) | copy-start | bytes 1572868
  165.6 13.5 %copy-start.38 = (f32[1,8,128,128]{3,2,1,0:T(8,128)S(1)}, f32[1,8,128,128]{3,2,1,0:T(8,128)}, u32[]{:S(2)}) copy-start(f32[1,8,128,128]{3,2,1,0:T(8,128)} %get-tuple-element.114) | copy-start | bytes 1572868
  173.7 14.0 %collective-permute-start.19 = (f32[256,512]{1,0:T(8,128)}, f32[256,512]{1,0:T(8,128)S(1)}, u32[]{:S(2)}, u32[]{:S(2)}) collective-permute-start(f32[256,512]{1,0:T(8,128)} %get-tuple-element.109), channel_id=1, source_target_pairs={{0,96},{16,112},{32,0},{48,16},{64,32},{80,48},{96,64},{112,80},{1... | collective-permute-start | bytes 1572872 | tf_op jit(solution)/shard_map/ppermute | solution.py:394
  176.1 11.6 %copy-start.4 = (f32[4,8,128,128]{3,2,1,0:T(8,128)S(1)}, f32[4,8,128,128]{3,2,1,0:T(8,128)}, u32[]{:S(2)}) copy-start(f32[4,8,128,128]{3,2,1,0:T(8,128)} %join_tiles.4) | copy-start | bytes 6291460
  176.1 13.2 %collective-permute-start.18 = (f32[256,512]{1,0:T(8,128)}, f32[256,512]{1,0:T(8,128)S(1)}, u32[]{:S(2)}, u32[]{:S(2)}) collective-permute-start(f32[256,512]{1,0:T(8,128)} %get-tuple-element.102), channel_id=1, source_target_pairs={{0,32},{16,48},{32,64},{48,80},{64,96},{80,112},{96,0},{112,16},{1... | collective-permute-start | bytes 1572872 | tf_op jit(solution)/shard_map/ppermute | solution.py:393
  176.1 22.4 %collective-permute-start.20 = (f32[1,8,128,128]{3,2,1,0:T(8,128)}, f32[1,8,128,128]{3,2,1,0:T(8,128)S(1)}, u32[]{:S(2)}, u32[]{:S(2)}) collective-permute-start(f32[1,8,128,128]{3,2,1,0:T(8,128)} %get-tuple-element.112), channel_id=1, source_target_pairs={{0,1},{1,2},{2,3},{3,0},{4,5},{5,6},{6,7},{7,4},{8,9},{9,10},{10,1... | collective-permute-start | bytes 1572872 | tf_op jit(solution)/shard_map/ppermute | solution.py:390
  178.0 2.9 copy-start.8
  178.0 20.5 %collective-permute-start.21 = (f32[1,8,128,128]{3,2,1,0:T(8,128)S(1)}, f32[1,8,128,128]{3,2,1,0:T(8,128)S(1)}, u32[]{:S(2)}, u32[]{:S(2)}) collective-permute-start(f32[1,8,128,128]{3,2,1,0:T(8,128)S(1)} %copy-done.39), channel_id=1, source_target_pairs={{0,2},{1,3},{2,0},{3,1},{4,6},{5,7},{6,4},{7,5},{8,10},{9,11},{10,... | collective-permute-start | bytes 1572872 | tf_op jit(solution)/shard_map/ppermute | solution.py:390
  179.0 1.8 copy-start.9
  179.1 19.4 %collective-permute-start.22 = (f32[1,8,128,128]{3,2,1,0:T(8,128)S(1)}, f32[1,8,128,128]{3,2,1,0:T(8,128)S(1)}, u32[]{:S(2)}, u32[]{:S(2)}) collective-permute-start(f32[1,8,128,128]{3,2,1,0:T(8,128)S(1)} %copy-done.38), channel_id=1, source_target_pairs={{0,3},{1,0},{2,1},{3,2},{4,7},{5,4},{6,5},{7,6},{8,11},{9,8},{10,9... | collective-permute-start | bytes 1572872 | tf_op jit(solution)/shard_map/ppermute | solution.py:390
  187.7 1.5 copy-start.20
  187.7 33.8 %collective-permute-start.23 = (f32[4,8,128,128]{3,2,1,0:T(8,128)S(1)}, f32[4,8,128,128]{3,2,1,0:T(8,128)S(1)}, u32[]{:S(2)}, u32[]{:S(2)}) collective-permute-start(f32[4,8,128,128]{3,2,1,0:T(8,128)S(1)} %copy-done.4), channel_id=1, source_target_pairs={{0,12},{1,13},{2,14},{3,15},{4,0},{5,1},{6,2},{7,3},{8,4},{9,5},{1... | collective-permute-start | bytes 6291464 | tf_op jit(solution)/shard_map/ppermute | solution.py:392
  204.3 39.6 %collective-permute-start.24 = (f32[4,8,128,128]{3,2,1,0:T(8,128)}, f32[4,8,128,128]{3,2,1,0:T(8,128)S(1)}, u32[]{:S(2)}, u32[]{:S(2)}) collective-permute-start(f32[4,8,128,128]{3,2,1,0:T(8,128)} %join_tiles.5), channel_id=1, source_target_pairs={{0,8},{1,9},{2,10},{3,11},{4,12},{5,13},{6,14},{7,15},{8,0},{9,1},... | collective-permute-start | bytes 6291464 | tf_op jit(solution)/shard_map/ppermute | solution.py:392
  206.7 45.6 %collective-permute-start.26 = (f32[512,512]{1,0:T(8,128)}, f32[512,512]{1,0:T(8,128)S(1)}, u32[]{:S(2)}, u32[]{:S(2)}) collective-permute-start(f32[512,512]{1,0:T(8,128)} %get-tuple-element.122), channel_id=1, source_target_pairs={{0,96},{16,112},{32,0},{48,16},{64,32},{80,48},{96,64},{112,80},{1... | collective-permute-start | bytes 3145736 | tf_op jit(solution)/shard_map/ppermute | solution.py:394
  209.4 42.9 %collective-permute-start.25 = (f32[512,512]{1,0:T(8,128)}, f32[512,512]{1,0:T(8,128)}, u32[]{:S(2)}, u32[]{:S(2)}) collective-permute-start(f32[512,512]{1,0:T(8,128)} %get-tuple-element.110), channel_id=1, source_target_pairs={{0,32},{16,48},{32,64},{48,80},{64,96},{80,112},{96,0},{112,16},{1... | collective-permute-start | bytes 3145736 | tf_op jit(solution)/shard_map/ppermute | solution.py:393
  209.4 42.8 %collective-permute-start.27 = (f32[256,512]{1,0:T(8,128)}, f32[256,512]{1,0:T(8,128)S(1)}, u32[]{:S(2)}, u32[]{:S(2)}) collective-permute-start(f32[256,512]{1,0:T(8,128)} %get-tuple-element.123), channel_id=1, source_target_pairs={{0,16},{16,0},{32,48},{48,32},{64,80},{80,64},{96,112},{112,96},{1... | collective-permute-start | bytes 1572872 | tf_op jit(solution)/shard_map/ppermute | solution.py:423
  229.6 34.2 %collective-permute-start.29 = (f32[256,512]{1,0:T(8,128)}, f32[256,512]{1,0:T(8,128)S(1)}, u32[]{:S(2)}, u32[]{:S(2)}) collective-permute-start(f32[256,512]{1,0:T(8,128)} %get-tuple-element.128), channel_id=1, source_target_pairs={{0,96},{16,112},{32,0},{48,16},{64,32},{80,48},{96,64},{112,80},{1... | collective-permute-start | bytes 1572872 | tf_op jit(solution)/shard_map/ppermute | solution.py:394
  244.0 19.9 %collective-permute-start.28 = (f32[256,512]{1,0:T(8,128)}, f32[256,512]{1,0:T(8,128)S(1)}, u32[]{:S(2)}, u32[]{:S(2)}) collective-permute-start(f32[256,512]{1,0:T(8,128)} %get-tuple-element.116), channel_id=1, source_target_pairs={{0,32},{16,48},{32,64},{48,80},{64,96},{80,112},{96,0},{112,16},{1... | collective-permute-start | bytes 1572872 | tf_op jit(solution)/shard_map/ppermute | solution.py:393
  252.2 8.8 %copy-start.43 = (f32[256,512]{1,0:T(8,128)S(1)}, f32[256,512]{1,0:T(8,128)}, u32[]{:S(2)}) copy-start(f32[256,512]{1,0:T(8,128)} %get-tuple-element.131) | copy-start | bytes 1572868
  252.2 22.7 %collective-permute-start.30 = (f32[256,512]{1,0:T(8,128)}, f32[256,512]{1,0:T(8,128)S(1)}, u32[]{:S(2)}, u32[]{:S(2)}) collective-permute-start(f32[256,512]{1,0:T(8,128)} %get-tuple-element.120), channel_id=1, source_target_pairs={{0,32},{16,48},{32,64},{48,80},{64,96},{80,112},{96,0},{112,16},{1... | collective-permute-start | bytes 1572872 | tf_op jit(solution)/shard_map/ppermute | solution.py:393
  260.9 13.9 %collective-permute-start.31 = (f32[256,512]{1,0:T(8,128)S(1)}, f32[256,512]{1,0:T(8,128)S(1)}, u32[]{:S(2)}, u32[]{:S(2)}) collective-permute-start(f32[256,512]{1,0:T(8,128)S(1)} %copy-done.43), channel_id=1, source_target_pairs={{0,96},{16,112},{32,0},{48,16},{64,32},{80,48},{96,64},{112,80},{1... | collective-permute-start | bytes 1572872 | tf_op jit(solution)/shard_map/ppermute | solution.py:394
  264.9 10.0 %copy-start.44 = (f32[256,512]{1,0:T(8,128)S(1)}, f32[256,512]{1,0:T(8,128)}, u32[]{:S(2)}) copy-start(f32[256,512]{1,0:T(8,128)} %get-tuple-element.136) | copy-start | bytes 1572868
  273.4 25.5 %collective-permute-start.35 = (f32[512,512]{1,0:T(8,128)}, f32[512,512]{1,0:T(8,128)S(1)}, u32[]{:S(2)}, u32[]{:S(2)}) collective-permute-start(f32[512,512]{1,0:T(8,128)} %get-tuple-element.135), channel_id=1, source_target_pairs={{0,96},{16,112},{32,0},{48,16},{64,32},{80,48},{96,64},{112,80},{1... | collective-permute-start | bytes 3145736 | tf_op jit(solution)/shard_map/ppermute | solution.py:394
  274.8 26.7 %collective-permute-start.34 = (f32[512,512]{1,0:T(8,128)}, f32[512,512]{1,0:T(8,128)S(1)}, u32[]{:S(2)}, u32[]{:S(2)}) collective-permute-start(f32[512,512]{1,0:T(8,128)} %get-tuple-element.129), channel_id=1, source_target_pairs={{0,32},{16,48},{32,64},{48,80},{64,96},{80,112},{96,0},{112,16},{1... | collective-permute-start | bytes 3145736 | tf_op jit(solution)/shard_map/ppermute | solution.py:393
  274.9 12.0 %collective-permute-start.36 = (f32[256,512]{1,0:T(8,128)S(1)}, f32[256,512]{1,0:T(8,128)S(1)}, u32[]{:S(2)}, u32[]{:S(2)}) collective-permute-start(f32[256,512]{1,0:T(8,128)S(1)} %copy-done.44), channel_id=1, source_target_pairs={{0,16},{16,0},{32,48},{48,32},{64,80},{80,64},{96,112},{112,96},{1... | collective-permute-start | bytes 1572872 | tf_op jit(solution)/shard_map/ppermute | solution.py:423
  284.3 32.9 %collective-permute-start.33 = (f32[512,512]{1,0:T(8,128)}, f32[512,512]{1,0:T(8,128)S(1)}, u32[]{:S(2)}, u32[]{:S(2)}) collective-permute-start(f32[512,512]{1,0:T(8,128)} %get-tuple-element.133), channel_id=1, source_target_pairs={{0,96},{16,112},{32,0},{48,16},{64,32},{80,48},{96,64},{112,80},{1... | collective-permute-start | bytes 3145736 | tf_op jit(solution)/shard_map/ppermute | solution.py:394
  286.9 33.2 %collective-permute-start.32 = (f32[512,512]{1,0:T(8,128)}, f32[512,512]{1,0:T(8,128)S(1)}, u32[]{:S(2)}, u32[]{:S(2)}) collective-permute-start(f32[512,512]{1,0:T(8,128)} %get-tuple-element.132), channel_id=1, source_target_pairs={{0,32},{16,48},{32,64},{48,80},{64,96},{80,112},{96,0},{112,16},{1... | collective-permute-start | bytes 3145736 | tf_op jit(solution)/shard_map/ppermute | solution.py:393
  286.9 14.6 %copy-start.24 = (f32[256,512]{1,0:T(8,128)}, f32[256,512]{1,0:T(8,128)S(1)}, u32[]{:S(2)}) copy-start(f32[256,512]{1,0:T(8,128)S(1)} %collective-permute-done.36.refs_6_) | copy-start | bytes 1572868
  298.9 2.6 copy-start.11
  310.0 10.1 %collective-permute-start.37 = (f32[256,512]{1,0:T(8,128)}, f32[256,512]{1,0:T(8,128)S(1)}, u32[]{:S(2)}, u32[]{:S(2)}) collective-permute-start(f32[256,512]{1,0:T(8,128)} %get-tuple-element.137), channel_id=1, source_target_pairs={{0,16},{16,0},{32,48},{48,32},{64,80},{80,64},{96,112},{112,96},{1... | collective-permute-start | bytes 1572872 | tf_op jit(solution)/shard_map/ppermute | solution.py:423
  317.2 2.9 copy-start.12
  321.2 9.9 %copy-start.2 = (s32[193]{0:T(256)S(1)}, s32[193]{0:T(256)}, u32[]{:S(2)}) copy-start(s32[193]{0:T(256)} %concatenate.3.table_ref) | copy-start | bytes 2320
  328.9 2.2 collective-permute-start.38
  (22 other events, 20.8 us)

commit v2 on v1

--- a/solution.py
+++ b/solution.py
@@ -52,7 +52,7 @@
 
 
 SMALL = pl.CostEstimate(flops=0, bytes_accessed=1024, transcendentals=0)
-BIG_MIB, SMALL_MIB = 56, 24
+BIG_MIB, SMALL_MIB = 24, 24
 
 
 def call(body, grid, table, args, in_specs, out_shape, out_specs, name, mib=BIG_MIB, **more):

time: 336 us -> 301 us (0.90)
  Pallas kernels: 120 us -> 56.1 us
  waiting for transfers between devices: 84.7 us -> 117 us
  starting transfers between devices: 56.8 us -> 68.8 us
  local copies, waits for them, and re-layouts: 16.4 us -> 4.5 us
    pallas_call x20, Pallas kernels: 120 us -> 56.1 us  [call(): pl.pallas_call(body, out_shape=out_shape, grid_spec=pltpu.PrefetchScalarG...]
    ppermute x4, starting transfers between devices: 8.68 us -> 20.2 us  [here(): return (result, (lax.ppermute(theirs, 'row', OTHER_CORE), at[f'theirs{t}']))]
    unnamed x94 -> x8, local copies, waits for them, and re-layouts: 14.7 us -> 3.39 us
    ppermute x3, waiting for transfers between devices: 15.1 us -> 25.6 us  [per_device(): lax.ppermute(array, ANYWHERE, plane_shift(False, t))]
    ppermute x12, waiting for transfers between devices: 14.1 us -> 21.4 us  [per_device(): lax.ppermute(a, ANYWHERE, plane_shift(True, s))]
    ppermute x8, waiting for transfers between devices: 8.64 us -> 15.1 us  [per_device(): up_z = lambda v: lax.ppermute(v, 'row', z_shift(1))]
    ppermute x8, waiting for transfers between devices: 28.9 us -> 34.3 us  [per_device(): down_z = lambda v: lax.ppermute(v, 'row', z_shift(-1))]
  transfers between devices with their start and end apart: 39 -> 39, of which waited for: 17 -> 19; matrix products, arithmetic and copies ran while one was open for 0% -> 0% of each run, Pallas kernels for 30% -> 16%
where the time goes in v2:
time: 301 us
  waiting for transfers between devices  117 us (39%)
  starting transfers between devices  68.8 us (23%)
  Pallas kernels  56.1 us (19%)
  blocking collectives  53.6 us (18%)
  local copies, waits for them, and re-layouts  4.5 us (1%)
    pallas_call x20, Pallas kernels, call(): pl.pallas_call(body, out_shape=out_shape, grid_spec=pltpu.PrefetchScalarG...  56.1 us
    all_to_all x1, blocking collectives, per_device(): own = lax.all_to_all(chosen, 'col', split_axis=0, concat_axis=0, tiled=True)  53.6 us
    ppermute x8, waiting for transfers between devices, per_device(): down_z = lambda v: lax.ppermute(v, 'row', z_shift(-1))  34.3 us
    ppermute x3, waiting for transfers between devices, per_device(): lax.ppermute(array, ANYWHERE, plane_shift(False, t))  25.6 us
    ppermute x12, waiting for transfers between devices, per_device(): lax.ppermute(a, ANYWHERE, plane_shift(True, s))  21.4 us
    ppermute x4, starting transfers between devices, here(): return (result, (lax.ppermute(theirs, 'row', OTHER_CORE), at[f'theirs{t}']))  20.2 us
    ppermute x8, starting transfers between devices, per_device(): down_z = lambda v: lax.ppermute(v, 'row', z_shift(-1))  18.2 us
    ppermute x3, waiting for transfers between devices, per_device(): lax.ppermute(amplitudes, 'row', z_shift(k))  15.8 us
  transfers between devices with their start and end apart: 39, of which 19 were waited for; matrix products, arithmetic and copies ran while one was open for 0% of the time, Pallas kernels for 16%

profile of v2, /device:TPU:3, one launch (start us, length us, event | category | flops | bytes accessed | tf_op | source)
XLA Modules:
  0.0 300.6 jit_solution(12779705622074811571)
XLA Ops:
  1.4 3.4 %copy-done = f32[128,1,1,128,128]{4,3,2,1,0:T(8,128)S(1)} copy-done((f32[128,1,1,128,128]{4,3,2,1,0:T(8,128)S(1)}, f32[128,1,1,128,128]{4,3,2,1,0:T(8,128)}, u32[]{:S(2)}) %copy-start) | copy-done | bytes 8388632
  4.7 1.0 pick_tiles.3
  5.8 1.4 collective-permute-start
  7.1 2.6 collective-permute-start.1
  9.8 1.1 collective-permute-start.2
  10.8 3.6 %collective-permute-start.4 = (f32[128,1024]{1,0:T(8,128)S(1)}, f32[128,1024]{1,0:T(8,128)S(1)}, u32[]{:S(2)}, u32[]{:S(2)}) collective-permute-start(f32[128,1024]{1,0:T(8,128)S(1)} %copy-done.1), channel_id=1, source_target_pairs={{0,64},{16,80},{32,96},{48,112},{64,0},{80,16},{96,32},{112,48},{1... | collective-permute-start | bytes 1572872 | tf_op jit(solution)/shard_map/ppermute | solution.py:397
  15.3 3.8 %collective-permute-start.5 = (f32[128,1024]{1,0:T(8,128)S(1)}, f32[128,1024]{1,0:T(8,128)S(1)}, u32[]{:S(2)}, u32[]{:S(2)}) collective-permute-start(f32[128,1024]{1,0:T(8,128)S(1)} %copy-done.1), channel_id=1, source_target_pairs={{0,96},{16,112},{32,0},{48,16},{64,32},{80,48},{96,64},{112,80},{1... | collective-permute-start | bytes 1572872 | tf_op jit(solution)/shard_map/ppermute | solution.py:397
  19.0 3.2 %collective-permute-done.1.refs_4_ = f32[1,8,128,128]{3,2,1,0:T(8,128)S(1)} collective-permute-done((f32[1,8,128,128]{3,2,1,0:T(8,128)S(1)}, f32[1,8,128,128]{3,2,1,0:T(8,128)S(1)}, u32[]{:S(2)}, u32[]{:S(2)}) %collective-permute-start.1) | collective-permute-done | bytes 524320 | tf_op jit(solution)/shard_map/ppermute | solution.py:390
  22.2 4.1 %collective-permute-done.4.refs_2_ = f32[128,1024]{1,0:T(8,128)S(1)} collective-permute-done((f32[128,1024]{1,0:T(8,128)S(1)}, f32[128,1024]{1,0:T(8,128)S(1)}, u32[]{:S(2)}, u32[]{:S(2)}) %collective-permute-start.4) | collective-permute-done | bytes 524320 | tf_op jit(solution)/shard_map/ppermute | solution.py:397
  26.4 11.7 %collective-permute-done.3.refs_1_ = f32[128,1024]{1,0:T(8,128)S(1)} collective-permute-done((f32[128,1024]{1,0:T(8,128)S(1)}, f32[128,1024]{1,0:T(8,128)S(1)}, u32[]{:S(2)}, u32[]{:S(2)}) %collective-permute-start.3) | collective-permute-done | bytes 524320 | tf_op jit(solution)/shard_map/ppermute | solution.py:397
  38.0 1.4 choose.1
  39.4 53.6 %all_to_all.5 = f32[16,128,512]{2,1,0:T(8,128)S(1)} all-to-all(f32[16,128,512]{2,1,0:T(8,128)S(1)} %choose.1), channel_id=1, replica_groups=mesh['row'=8,'col'=16] {'col'}, dimensions={0} | all-to-all | bytes 8388608 | tf_op jit(solution)/shard_map/all_to_all | solution.py:402
  93.0 2.0 collective-permute-start.6
  95.0 0.9 pick_tiles.4
  96.0 1.7 collective-permute-start.8
  97.8 0.9 collective-permute-start.9
  98.7 3.1 %collective-permute-done.6.refs_1_ = f32[2048,512]{1,0:T(8,128)S(1)} collective-permute-done((f32[2048,512]{1,0:T(8,128)S(1)}, f32[2048,512]{1,0:T(8,128)S(1)}, u32[]{:S(2)}, u32[]{:S(2)}) %collective-permute-start.6) | collective-permute-done | bytes 4194336 | tf_op jit(solution)/shard_map/ppermute | solution.py:404
  101.8 3.1 %products_away.4 = (f32[256,512]{1,0:T(8,128)S(1)}, f32[256,512]{1,0:T(8,128)S(1)}, bf16[1024,512]{1,0:T(8,128)(2,1)S(1)}, bf16[1024,512]{1,0:T(8,128)(2,1)S(1)}) custom-call(s32[193]{0:T(256)S(1)} %concatenate.3.table_ref, f32[2048,512]{1,0:T(8,128)S(1)} %bitcast.86, f32[2048,512]{1,0:T(8,128)S(1)} %collective-permute-done.6.refs_1_, ...), custom_call_target="tpu_custom_call" | custom-call | bytes 1024 | tf_op jit(solution)/shard_map/products_away/pallas_call | solution.py:60
  104.9 1.3 pick_tiles.5
  106.2 4.7 %collective-permute-done.7.refs_0_ = f32[1,8,128,128]{3,2,1,0:T(8,128)S(1)} collective-permute-done((f32[1,8,128,128]{3,2,1,0:T(8,128)S(1)}, f32[1,8,128,128]{3,2,1,0:T(8,128)S(1)}, u32[]{:S(2)}, u32[]{:S(2)}) %collective-permute-start.7) | collective-permute-done | bytes 524320 | tf_op jit(solution)/shard_map/ppermute | solution.py:390
  110.9 0.9 collective-permute-done.9.refs_2_
  111.8 0.9 join_tiles.3
  112.7 2.5 collective-permute-start.11
  115.7 9.5 %collective-permute-done.11.refs_5_ = f32[256,512]{1,0:T(8,128)S(1)} collective-permute-done((f32[256,512]{1,0:T(8,128)S(1)}, f32[256,512]{1,0:T(8,128)S(1)}, u32[]{:S(2)}, u32[]{:S(2)}) %collective-permute-start.11) | collective-permute-done | bytes 524320 | tf_op jit(solution)/shard_map/ppermute | solution.py:394
  125.2 3.1 %collective-permute-done.10.refs_4_ = f32[256,512]{1,0:T(8,128)S(1)} collective-permute-done((f32[256,512]{1,0:T(8,128)S(1)}, f32[256,512]{1,0:T(8,128)S(1)}, u32[]{:S(2)}, u32[]{:S(2)}) %collective-permute-start.10) | collective-permute-done | bytes 524320 | tf_op jit(solution)/shard_map/ppermute | solution.py:393
  128.3 4.8 %products_next.4 = (f32[512,512]{1,0:T(8,128)S(1)}, f32[512,512]{1,0:T(8,128)S(1)}) custom-call(s32[193]{0:T(256)S(1)} %concatenate.3.table_ref, f32[2048,512]{1,0:T(8,128)S(1)} %bitcast.87, f32[2048,512]{1,0:T(8,128)S(1)} %collective-permute-done.6.refs_1_, bf16[1024,512]{1,0:T(8,128)(2,1)S(1)} %get-tuple-element.93.refs_2_, ...), custom_call_target="tpu_custom_call" | custom-call | bytes 1024 | tf_op jit(solution)/shard_map/products_next/pallas_call | solution.py:60
  133.4 1.2 collective-permute-start.16
  135.1 2.2 collective-permute-start.14
  137.3 12.5 %collective-permute-done.13.refs_1_ = f32[1,8,128,128]{3,2,1,0:T(8,128)S(1)} collective-permute-done((f32[1,8,128,128]{3,2,1,0:T(8,128)S(1)}, f32[1,8,128,128]{3,2,1,0:T(8,128)S(1)}, u32[]{:S(2)}, u32[]{:S(2)}) %collective-permute-start.13) | collective-permute-done | bytes 524320 | tf_op jit(solution)/shard_map/ppermute | solution.py:390
  149.8 0.9 join_tiles.4
  150.7 3.1 %products_away.5 = (f32[256,512]{1,0:T(8,128)S(1)}, f32[256,512]{1,0:T(8,128)S(1)}, bf16[1024,512]{1,0:T(8,128)(2,1)S(1)}, bf16[1024,512]{1,0:T(8,128)(2,1)S(1)}) custom-call(s32[193]{0:T(256)S(1)} %concatenate.3.table_ref, f32[2048,512]{1,0:T(8,128)S(1)} %bitcast.88, f32[2048,512]{1,0:T(8,128)S(1)} %collective-permute-done.6.refs_1_, ...), custom_call_target="tpu_custom_call" | custom-call | bytes 1024 | tf_op jit(solution)/shard_map/products_away/pallas_call | solution.py:60
  153.8 1.8 collective-permute-start.19
  156.1 2.4 collective-permute-start.21
  158.8 3.4 %products_here.4 = (f32[256,512]{1,0:T(8,128)S(1)}, f32[256,4096]{1,0:T(8,128)}) custom-call(s32[193]{0:T(256)S(1)} %concatenate.3.table_ref, f32[2048,512]{1,0:T(8,128)S(1)} %bitcast.89, f32[2048,512]{1,0:T(8,128)S(1)} %collective-permute-done.6.refs_1_, bf16[1024,512]{1,0:T(8,128)(2,1)S(1)} %get-tuple-element.93.refs_2_, ...), custom_call_target="tpu_custom_call" | custom-call | bytes 1024 | tf_op jit(solution)/shard_map/products_here/pallas_call | solution.py:60
  162.2 4.2 %collective-permute-done.19.refs_5_ = f32[256,512]{1,0:T(8,128)S(1)} collective-permute-done((f32[256,512]{1,0:T(8,128)S(1)}, f32[256,512]{1,0:T(8,128)S(1)}, u32[]{:S(2)}, u32[]{:S(2)}) %collective-permute-start.19) | collective-permute-done | bytes 524320 | tf_op jit(solution)/shard_map/ppermute | solution.py:394
  166.4 2.0 collective-permute-start.23
  168.5 4.8 %products_next.5 = (f32[512,512]{1,0:T(8,128)S(1)}, f32[512,512]{1,0:T(8,128)S(1)}) custom-call(s32[193]{0:T(256)S(1)} %concatenate.3.table_ref, f32[2048,512]{1,0:T(8,128)S(1)} %bitcast.90, f32[2048,512]{1,0:T(8,128)S(1)} %collective-permute-done.6.refs_1_, bf16[1024,512]{1,0:T(8,128)(2,1)S(1)} %get-tuple-element.107.refs_2_, ...), custom_call_target="tpu_custom_call" | custom-call | bytes 1024 | tf_op jit(solution)/shard_map/products_next/pallas_call | solution.py:60
  173.3 0.9 join_tiles.5
  174.1 2.2 collective-permute-start.24
  176.4 2.0 collective-permute-start.26
  178.4 11.9 %collective-permute-start.27 = (f32[256,512]{1,0:T(8,128)S(1)}, f32[256,512]{1,0:T(8,128)S(1)}, u32[]{:S(2)}, u32[]{:S(2)}) collective-permute-start(f32[256,512]{1,0:T(8,128)S(1)} %get-tuple-element.123), channel_id=1, source_target_pairs={{0,16},{16,0},{32,48},{48,32},{64,80},{80,64},{96,112},{112,96},{1... | collective-permute-start | bytes 1572872 | tf_op jit(solution)/shard_map/ppermute | solution.py:423
  190.2 9.0 %collective-permute-done.23.refs_2_ = f32[4,8,128,128]{3,2,1,0:T(8,128)S(1)} collective-permute-done((f32[4,8,128,128]{3,2,1,0:T(8,128)S(1)}, f32[4,8,128,128]{3,2,1,0:T(8,128)S(1)}, u32[]{:S(2)}, u32[]{:S(2)}) %collective-permute-start.23) | collective-permute-done | bytes 2097184 | tf_op jit(solution)/shard_map/ppermute | solution.py:392
  199.2 3.1 %products_away.6 = (f32[256,512]{1,0:T(8,128)S(1)}, f32[256,512]{1,0:T(8,128)S(1)}, bf16[1024,512]{1,0:T(8,128)(2,1)S(1)}, bf16[1024,512]{1,0:T(8,128)(2,1)S(1)}) custom-call(s32[193]{0:T(256)S(1)} %concatenate.3.table_ref, f32[2048,512]{1,0:T(8,128)S(1)} %bitcast.91, f32[2048,512]{1,0:T(8,128)S(1)} %collective-permute-done.6.refs_1_, ...), custom_call_target="tpu_custom_call" | custom-call | bytes 1024 | tf_op jit(solution)/shard_map/products_away/pallas_call | solution.py:60
  202.3 2.5 collective-permute-start.29
  204.8 16.6 %collective-permute-done.24.refs_2_ = f32[4,8,128,128]{3,2,1,0:T(8,128)S(1)} collective-permute-done((f32[4,8,128,128]{3,2,1,0:T(8,128)S(1)}, f32[4,8,128,128]{3,2,1,0:T(8,128)S(1)}, u32[]{:S(2)}, u32[]{:S(2)}) %collective-permute-start.24) | collective-permute-done | bytes 2097184 | tf_op jit(solution)/shard_map/ppermute | solution.py:392
  221.4 3.1 %products_away.7 = (f32[256,512]{1,0:T(8,128)S(1)}, f32[256,512]{1,0:T(8,128)S(1)}, bf16[1024,512]{1,0:T(8,128)(2,1)S(1)}, bf16[1024,512]{1,0:T(8,128)(2,1)S(1)}) custom-call(s32[193]{0:T(256)S(1)} %concatenate.3.table_ref, f32[2048,512]{1,0:T(8,128)S(1)} %bitcast.92, f32[2048,512]{1,0:T(8,128)S(1)} %collective-permute-done.6.refs_1_, ...), custom_call_target="tpu_custom_call" | custom-call | bytes 1024 | tf_op jit(solution)/shard_map/products_away/pallas_call | solution.py:60
  225.0 4.3 %products_here.5 = (f32[256,512]{1,0:T(8,128)S(1)}, f32[256,4096]{1,0:T(8,128)}) custom-call(s32[193]{0:T(256)S(1)} %concatenate.3.table_ref, f32[2048,512]{1,0:T(8,128)S(1)} %bitcast.93, f32[2048,512]{1,0:T(8,128)S(1)} %collective-permute-done.6.refs_1_, bf16[1024,512]{1,0:T(8,128)(2,1)S(1)} %get-tuple-element.107.refs_2_, ...), custom_call_target="tpu_custom_call", output_to_operand_aliasing={{1}: (8, {})} | custom-call | bytes 1024 | tf_op jit(solution)/shard_map/products_here/pallas_call | solution.py:60
  229.3 2.4 collective-permute-start.31
  231.7 2.3 collective-permute-done.28.refs_4_
  234.0 4.8 %products_next.6 = (f32[512,512]{1,0:T(8,128)S(1)}, f32[512,512]{1,0:T(8,128)S(1)}) custom-call(s32[193]{0:T(256)S(1)} %concatenate.3.table_ref, f32[2048,512]{1,0:T(8,128)S(1)} %bitcast.94, f32[2048,512]{1,0:T(8,128)S(1)} %collective-permute-done.6.refs_1_, bf16[1024,512]{1,0:T(8,128)(2,1)S(1)} %get-tuple-element.126.refs_2_, ...), custom_call_target="tpu_custom_call" | custom-call | bytes 1024 | tf_op jit(solution)/shard_map/products_next/pallas_call | solution.py:60
  238.8 3.9 %collective-permute-start.35 = (f32[512,512]{1,0:T(8,128)S(1)}, f32[512,512]{1,0:T(8,128)S(1)}, u32[]{:S(2)}, u32[]{:S(2)}) collective-permute-start(f32[512,512]{1,0:T(8,128)S(1)} %get-tuple-element.135), channel_id=1, source_target_pairs={{0,96},{16,112},{32,0},{48,16},{64,32},{80,48},{96,64},{112,80},{1... | collective-permute-start | bytes 3145736 | tf_op jit(solution)/shard_map/ppermute | solution.py:394
  242.6 3.8 %collective-permute-start.36 = (f32[256,512]{1,0:T(8,128)S(1)}, f32[256,512]{1,0:T(8,128)S(1)}, u32[]{:S(2)}, u32[]{:S(2)}) collective-permute-start(f32[256,512]{1,0:T(8,128)S(1)} %get-tuple-element.136), channel_id=1, source_target_pairs={{0,16},{16,0},{32,48},{48,32},{64,80},{80,64},{96,112},{112,96},{1... | collective-permute-start | bytes 1572872 | tf_op jit(solution)/shard_map/ppermute | solution.py:423
  246.4 4.8 %products_next.7 = (f32[512,512]{1,0:T(8,128)S(1)}, f32[512,512]{1,0:T(8,128)S(1)}) custom-call(s32[193]{0:T(256)S(1)} %concatenate.3.table_ref, f32[2048,512]{1,0:T(8,128)S(1)} %bitcast.95, f32[2048,512]{1,0:T(8,128)S(1)} %collective-permute-done.6.refs_1_, bf16[1024,512]{1,0:T(8,128)(2,1)S(1)} %get-tuple-element.118.refs_2_, ...), custom_call_target="tpu_custom_call" | custom-call | bytes 1024 | tf_op jit(solution)/shard_map/products_next/pallas_call | solution.py:60
  251.2 2.9 collective-permute-start.33
  254.1 10.2 %collective-permute-done.35.refs_5_ = f32[512,512]{1,0:T(8,128)S(1)} collective-permute-done((f32[512,512]{1,0:T(8,128)S(1)}, f32[512,512]{1,0:T(8,128)S(1)}, u32[]{:S(2)}, u32[]{:S(2)}) %collective-permute-start.35) | collective-permute-done | bytes 1048608 | tf_op jit(solution)/shard_map/ppermute | solution.py:394
  264.3 4.8 %collective-permute-done.34.refs_4_ = f32[512,512]{1,0:T(8,128)S(1)} collective-permute-done((f32[512,512]{1,0:T(8,128)S(1)}, f32[512,512]{1,0:T(8,128)S(1)}, u32[]{:S(2)}, u32[]{:S(2)}) %collective-permute-start.34) | collective-permute-done | bytes 1048608 | tf_op jit(solution)/shard_map/ppermute | solution.py:393
  269.1 4.3 %products_here.6 = (f32[256,512]{1,0:T(8,128)S(1)}, f32[256,4096]{1,0:T(8,128)}) custom-call(s32[193]{0:T(256)S(1)} %concatenate.3.table_ref, f32[2048,512]{1,0:T(8,128)S(1)} %bitcast.96, f32[2048,512]{1,0:T(8,128)S(1)} %collective-permute-done.6.refs_1_, bf16[1024,512]{1,0:T(8,128)(2,1)S(1)} %get-tuple-element.126.refs_2_, ...), custom_call_target="tpu_custom_call", output_to_operand_aliasing={{1}: (8, {})} | custom-call | bytes 1024 | tf_op jit(solution)/shard_map/products_here/pallas_call | solution.py:60
  273.3 2.9 collective-permute-start.37
  276.2 10.5 %collective-permute-done.33.refs_5_ = f32[512,512]{1,0:T(8,128)S(1)} collective-permute-done((f32[512,512]{1,0:T(8,128)S(1)}, f32[512,512]{1,0:T(8,128)S(1)}, u32[]{:S(2)}, u32[]{:S(2)}) %collective-permute-start.33) | collective-permute-done | bytes 1048608 | tf_op jit(solution)/shard_map/ppermute | solution.py:394
  286.7 4.8 %collective-permute-done.32.refs_4_ = f32[512,512]{1,0:T(8,128)S(1)} collective-permute-done((f32[512,512]{1,0:T(8,128)S(1)}, f32[512,512]{1,0:T(8,128)S(1)}, u32[]{:S(2)}, u32[]{:S(2)}) %collective-permute-start.32) | collective-permute-done | bytes 1048608 | tf_op jit(solution)/shard_map/ppermute | solution.py:393
  291.6 4.3 %products_here.7 = (f32[256,512]{1,0:T(8,128)S(1)}, f32[256,4096]{1,0:T(8,128)}) custom-call(s32[193]{0:T(256)S(1)} %concatenate.3.table_ref, f32[2048,512]{1,0:T(8,128)S(1)} %bitcast.97, f32[2048,512]{1,0:T(8,128)S(1)} %collective-permute-done.6.refs_1_, bf16[1024,512]{1,0:T(8,128)(2,1)S(1)} %get-tuple-element.118.refs_2_, ...), custom_call_target="tpu_custom_call", output_to_operand_aliasing={{1}: (8, {})} | custom-call | bytes 1024 | tf_op jit(solution)/shard_map/products_here/pallas_call | solution.py:60
  295.8 1.7 collective-permute-start.38
  297.5 1.5 collective-permute-done.38.theirs_ref
  299.1 1.4 place.1
  (53 shorter events, 4.9 us)
Async XLA Ops:
  1.4 3.4 %copy-start = (f32[128,1,1,128,128]{4,3,2,1,0:T(8,128)S(1)}, f32[128,1,1,128,128]{4,3,2,1,0:T(8,128)}, u32[]{:S(2)}) copy-start(f32[128,1,1,128,128]{4,3,2,1,0:T(8,128)} %param.4) | copy-start | bytes 25165828
  4.7 6.1 %copy-start.1 = (f32[128,1024]{1,0:T(8,128)S(1)}, f32[128,1024]{1,0:T(8,128)}, u32[]{:S(2)}) copy-start(f32[128,1024]{1,0:T(8,128)} %refs_0_.1) | copy-start | bytes 1572868
  4.7 90.3 %slice-start = ((s8[8388608]{0:T(1024)(128)(4,1)}), s8[4194304]{0:T(1024)(128)(4,1)S(1)}, s32[]{:S(2)}) async-start(s8[8388608]{0:T(1024)(128)(4,1)} %bitcast.99), calls=%async_computation.1 | async-start | bytes 8388608
  5.8 9.5 %collective-permute-start = (f32[1,8,128,128]{3,2,1,0:T(8,128)S(1)}, f32[1,8,128,128]{3,2,1,0:T(8,128)S(1)}, u32[]{:S(2)}, u32[]{:S(2)}) collective-permute-start(f32[1,8,128,128]{3,2,1,0:T(8,128)S(1)} %get-tuple-element.74), channel_id=1, source_target_pairs={{0,1},{1,2},{2,3},{3,0},{4,5},{5,6},{6,7},{7,4},{8,9},{9,10},{10,1... | collective-permute-start | bytes 1572872 | tf_op jit(solution)/shard_map/ppermute | solution.py:390
  7.1 15.1 %collective-permute-start.1 = (f32[1,8,128,128]{3,2,1,0:T(8,128)S(1)}, f32[1,8,128,128]{3,2,1,0:T(8,128)S(1)}, u32[]{:S(2)}, u32[]{:S(2)}) collective-permute-start(f32[1,8,128,128]{3,2,1,0:T(8,128)S(1)} %get-tuple-element.75), channel_id=1, source_target_pairs={{0,2},{1,3},{2,0},{3,1},{4,6},{5,7},{6,4},{7,5},{8,10},{9,11},{10,... | collective-permute-start | bytes 1572872 | tf_op jit(solution)/shard_map/ppermute | solution.py:390
  9.8 12.5 %collective-permute-start.2 = (f32[1,8,128,128]{3,2,1,0:T(8,128)S(1)}, f32[1,8,128,128]{3,2,1,0:T(8,128)S(1)}, u32[]{:S(2)}, u32[]{:S(2)}) collective-permute-start(f32[1,8,128,128]{3,2,1,0:T(8,128)S(1)} %get-tuple-element.76), channel_id=1, source_target_pairs={{0,3},{1,0},{2,1},{3,2},{4,7},{5,4},{6,5},{7,6},{8,11},{9,8},{10,9... | collective-permute-start | bytes 1572872 | tf_op jit(solution)/shard_map/ppermute | solution.py:390
  10.8 15.5 %collective-permute-start.4 = (f32[128,1024]{1,0:T(8,128)S(1)}, f32[128,1024]{1,0:T(8,128)S(1)}, u32[]{:S(2)}, u32[]{:S(2)}) collective-permute-start(f32[128,1024]{1,0:T(8,128)S(1)} %copy-done.1), channel_id=1, source_target_pairs={{0,64},{16,80},{32,96},{48,112},{64,0},{80,16},{96,32},{112,48},{1... | collective-permute-start | bytes 1572872 | tf_op jit(solution)/shard_map/ppermute | solution.py:397
  14.4 23.6 %collective-permute-start.3 = (f32[128,1024]{1,0:T(8,128)S(1)}, f32[128,1024]{1,0:T(8,128)S(1)}, u32[]{:S(2)}, u32[]{:S(2)}) collective-permute-start(f32[128,1024]{1,0:T(8,128)S(1)} %copy-done.1), channel_id=1, source_target_pairs={{0,32},{16,48},{32,64},{48,80},{64,96},{80,112},{96,0},{112,16},{1... | collective-permute-start | bytes 1572872 | tf_op jit(solution)/shard_map/ppermute | solution.py:397
  15.3 22.8 %collective-permute-start.5 = (f32[128,1024]{1,0:T(8,128)S(1)}, f32[128,1024]{1,0:T(8,128)S(1)}, u32[]{:S(2)}, u32[]{:S(2)}) collective-permute-start(f32[128,1024]{1,0:T(8,128)S(1)} %copy-done.1), channel_id=1, source_target_pairs={{0,96},{16,112},{32,0},{48,16},{64,32},{80,48},{96,64},{112,80},{1... | collective-permute-start | bytes 1572872 | tf_op jit(solution)/shard_map/ppermute | solution.py:397
  22.2 72.8 %slice-start.1 = ((s8[8388608]{0:T(1024)(128)(4,1)}), s8[4194304]{0:T(1024)(128)(4,1)S(1)}, s32[]{:S(2)}) async-start(s8[8388608]{0:T(1024)(128)(4,1)} %bitcast.99), calls=%async_computation.2 | async-start | bytes 8388608
  93.0 8.8 %collective-permute-start.6 = (f32[2048,512]{1,0:T(8,128)S(1)}, f32[2048,512]{1,0:T(8,128)S(1)}, u32[]{:S(2)}, u32[]{:S(2)}) collective-permute-start(f32[2048,512]{1,0:T(8,128)S(1)} %bitcast.85), channel_id=1, source_target_pairs={{0,16},{16,0},{32,48},{48,32},{64,80},{80,64},{96,112},{112,96},{1... | collective-permute-start | bytes 12582920 | tf_op jit(solution)/shard_map/ppermute | solution.py:404
  95.9 14.9 %collective-permute-start.7 = (f32[1,8,128,128]{3,2,1,0:T(8,128)S(1)}, f32[1,8,128,128]{3,2,1,0:T(8,128)S(1)}, u32[]{:S(2)}, u32[]{:S(2)}) collective-permute-start(f32[1,8,128,128]{3,2,1,0:T(8,128)S(1)} %get-tuple-element.79), channel_id=1, source_target_pairs={{0,1},{1,2},{2,3},{3,0},{4,5},{5,6},{6,7},{7,4},{8,9},{9,10},{10,1... | collective-permute-start | bytes 1572872 | tf_op jit(solution)/shard_map/ppermute | solution.py:390
  96.0 14.8 %collective-permute-start.8 = (f32[1,8,128,128]{3,2,1,0:T(8,128)S(1)}, f32[1,8,128,128]{3,2,1,0:T(8,128)S(1)}, u32[]{:S(2)}, u32[]{:S(2)}) collective-permute-start(f32[1,8,128,128]{3,2,1,0:T(8,128)S(1)} %get-tuple-element.80), channel_id=1, source_target_pairs={{0,2},{1,3},{2,0},{3,1},{4,6},{5,7},{6,4},{7,5},{8,10},{9,11},{10,... | collective-permute-start | bytes 1572872 | tf_op jit(solution)/shard_map/ppermute | solution.py:390
  97.8 14.0 %collective-permute-start.9 = (f32[1,8,128,128]{3,2,1,0:T(8,128)S(1)}, f32[1,8,128,128]{3,2,1,0:T(8,128)S(1)}, u32[]{:S(2)}, u32[]{:S(2)}) collective-permute-start(f32[1,8,128,128]{3,2,1,0:T(8,128)S(1)} %get-tuple-element.81), channel_id=1, source_target_pairs={{0,3},{1,0},{2,1},{3,2},{4,7},{5,4},{6,5},{7,6},{8,11},{9,8},{10,9... | collective-permute-start | bytes 1572872 | tf_op jit(solution)/shard_map/ppermute | solution.py:390
  112.7 38.1 %collective-permute-start.15 = (f32[4,8,128,128]{3,2,1,0:T(8,128)S(1)}, f32[4,8,128,128]{3,2,1,0:T(8,128)S(1)}, u32[]{:S(2)}, u32[]{:S(2)}) collective-permute-start(f32[4,8,128,128]{3,2,1,0:T(8,128)S(1)} %join_tiles.3), channel_id=1, source_target_pairs={{0,4},{1,5},{2,6},{3,7},{4,8},{5,9},{6,10},{7,11},{8,12},{9,13},{1... | collective-permute-start | bytes 6291464 | tf_op jit(solution)/shard_map/ppermute | solution.py:392
  112.7 12.4 %collective-permute-start.11 = (f32[256,512]{1,0:T(8,128)S(1)}, f32[256,512]{1,0:T(8,128)S(1)}, u32[]{:S(2)}, u32[]{:S(2)}) collective-permute-start(f32[256,512]{1,0:T(8,128)S(1)} %get-tuple-element.95), channel_id=1, source_target_pairs={{0,96},{16,112},{32,0},{48,16},{64,32},{80,48},{96,64},{112,80},{1... | collective-permute-start | bytes 1572872 | tf_op jit(solution)/shard_map/ppermute | solution.py:394
  115.3 13.1 %collective-permute-start.10 = (f32[256,512]{1,0:T(8,128)S(1)}, f32[256,512]{1,0:T(8,128)S(1)}, u32[]{:S(2)}, u32[]{:S(2)}) collective-permute-start(f32[256,512]{1,0:T(8,128)S(1)} %get-tuple-element.83), channel_id=1, source_target_pairs={{0,32},{16,48},{32,64},{48,80},{64,96},{80,112},{96,0},{112,16},{1... | collective-permute-start | bytes 1572872 | tf_op jit(solution)/shard_map/ppermute | solution.py:393
  115.3 19.9 %collective-permute-start.12 = (f32[1,8,128,128]{3,2,1,0:T(8,128)S(1)}, f32[1,8,128,128]{3,2,1,0:T(8,128)S(1)}, u32[]{:S(2)}, u32[]{:S(2)}) collective-permute-start(f32[1,8,128,128]{3,2,1,0:T(8,128)S(1)} %get-tuple-element.98), channel_id=1, source_target_pairs={{0,1},{1,2},{2,3},{3,0},{4,5},{5,6},{6,7},{7,4},{8,9},{9,10},{10,1... | collective-permute-start | bytes 1572872 | tf_op jit(solution)/shard_map/ppermute | solution.py:390
  133.1 23.0 %collective-permute-start.17 = (f32[512,512]{1,0:T(8,128)S(1)}, f32[512,512]{1,0:T(8,128)S(1)}, u32[]{:S(2)}, u32[]{:S(2)}) collective-permute-start(f32[512,512]{1,0:T(8,128)S(1)} %get-tuple-element.104), channel_id=1, source_target_pairs={{0,96},{16,112},{32,0},{48,16},{64,32},{80,48},{96,64},{112,80},{1... | collective-permute-start | bytes 3145736 | tf_op jit(solution)/shard_map/ppermute | solution.py:394
  133.4 25.0 %collective-permute-start.16 = (f32[512,512]{1,0:T(8,128)S(1)}, f32[512,512]{1,0:T(8,128)S(1)}, u32[]{:S(2)}, u32[]{:S(2)}) collective-permute-start(f32[512,512]{1,0:T(8,128)S(1)} %get-tuple-element.96), channel_id=1, source_target_pairs={{0,32},{16,48},{32,64},{48,80},{64,96},{80,112},{96,0},{112,16},{1... | collective-permute-start | bytes 3145736 | tf_op jit(solution)/shard_map/ppermute | solution.py:393
  134.6 15.2 %collective-permute-start.13 = (f32[1,8,128,128]{3,2,1,0:T(8,128)S(1)}, f32[1,8,128,128]{3,2,1,0:T(8,128)S(1)}, u32[]{:S(2)}, u32[]{:S(2)}) collective-permute-start(f32[1,8,128,128]{3,2,1,0:T(8,128)S(1)} %get-tuple-element.99), channel_id=1, source_target_pairs={{0,2},{1,3},{2,0},{3,1},{4,6},{5,7},{6,4},{7,5},{8,10},{9,11},{10,... | collective-permute-start | bytes 1572872 | tf_op jit(solution)/shard_map/ppermute | solution.py:390
  135.1 14.7 %collective-permute-start.14 = (f32[1,8,128,128]{3,2,1,0:T(8,128)S(1)}, f32[1,8,128,128]{3,2,1,0:T(8,128)S(1)}, u32[]{:S(2)}, u32[]{:S(2)}) collective-permute-start(f32[1,8,128,128]{3,2,1,0:T(8,128)S(1)} %get-tuple-element.100), channel_id=1, source_target_pairs={{0,3},{1,0},{2,1},{3,2},{4,7},{5,4},{6,5},{7,6},{8,11},{9,8},{10,9... | collective-permute-start | bytes 1572872 | tf_op jit(solution)/shard_map/ppermute | solution.py:390
  153.8 12.6 %collective-permute-start.19 = (f32[256,512]{1,0:T(8,128)S(1)}, f32[256,512]{1,0:T(8,128)S(1)}, u32[]{:S(2)}, u32[]{:S(2)}) collective-permute-start(f32[256,512]{1,0:T(8,128)S(1)} %get-tuple-element.109), channel_id=1, source_target_pairs={{0,96},{16,112},{32,0},{48,16},{64,32},{80,48},{96,64},{112,80},{1... | collective-permute-start | bytes 1572872 | tf_op jit(solution)/shard_map/ppermute | solution.py:394
  155.6 12.9 %collective-permute-start.18 = (f32[256,512]{1,0:T(8,128)S(1)}, f32[256,512]{1,0:T(8,128)S(1)}, u32[]{:S(2)}, u32[]{:S(2)}) collective-permute-start(f32[256,512]{1,0:T(8,128)S(1)} %get-tuple-element.102), channel_id=1, source_target_pairs={{0,32},{16,48},{32,64},{48,80},{64,96},{80,112},{96,0},{112,16},{1... | collective-permute-start | bytes 1572872 | tf_op jit(solution)/shard_map/ppermute | solution.py:393
  155.6 17.7 %collective-permute-start.20 = (f32[1,8,128,128]{3,2,1,0:T(8,128)S(1)}, f32[1,8,128,128]{3,2,1,0:T(8,128)S(1)}, u32[]{:S(2)}, u32[]{:S(2)}) collective-permute-start(f32[1,8,128,128]{3,2,1,0:T(8,128)S(1)} %get-tuple-element.112), channel_id=1, source_target_pairs={{0,1},{1,2},{2,3},{3,0},{4,5},{5,6},{6,7},{7,4},{8,9},{9,10},{10,1... | collective-permute-start | bytes 1572872 | tf_op jit(solution)/shard_map/ppermute | solution.py:390
  156.1 17.1 %collective-permute-start.21 = (f32[1,8,128,128]{3,2,1,0:T(8,128)S(1)}, f32[1,8,128,128]{3,2,1,0:T(8,128)S(1)}, u32[]{:S(2)}, u32[]{:S(2)}) collective-permute-start(f32[1,8,128,128]{3,2,1,0:T(8,128)S(1)} %get-tuple-element.113), channel_id=1, source_target_pairs={{0,2},{1,3},{2,0},{3,1},{4,6},{5,7},{6,4},{7,5},{8,10},{9,11},{10,... | collective-permute-start | bytes 1572872 | tf_op jit(solution)/shard_map/ppermute | solution.py:390
  158.5 14.8 %collective-permute-start.22 = (f32[1,8,128,128]{3,2,1,0:T(8,128)S(1)}, f32[1,8,128,128]{3,2,1,0:T(8,128)S(1)}, u32[]{:S(2)}, u32[]{:S(2)}) collective-permute-start(f32[1,8,128,128]{3,2,1,0:T(8,128)S(1)} %get-tuple-element.114), channel_id=1, source_target_pairs={{0,3},{1,0},{2,1},{3,2},{4,7},{5,4},{6,5},{7,6},{8,11},{9,8},{10,9... | collective-permute-start | bytes 1572872 | tf_op jit(solution)/shard_map/ppermute | solution.py:390
  166.4 32.8 %collective-permute-start.23 = (f32[4,8,128,128]{3,2,1,0:T(8,128)S(1)}, f32[4,8,128,128]{3,2,1,0:T(8,128)S(1)}, u32[]{:S(2)}, u32[]{:S(2)}) collective-permute-start(f32[4,8,128,128]{3,2,1,0:T(8,128)S(1)} %join_tiles.4), channel_id=1, source_target_pairs={{0,12},{1,13},{2,14},{3,15},{4,0},{5,1},{6,2},{7,3},{8,4},{9,5},{1... | collective-permute-start | bytes 6291464 | tf_op jit(solution)/shard_map/ppermute | solution.py:392
  174.1 47.3 %collective-permute-start.24 = (f32[4,8,128,128]{3,2,1,0:T(8,128)S(1)}, f32[4,8,128,128]{3,2,1,0:T(8,128)S(1)}, u32[]{:S(2)}, u32[]{:S(2)}) collective-permute-start(f32[4,8,128,128]{3,2,1,0:T(8,128)S(1)} %join_tiles.5), channel_id=1, source_target_pairs={{0,8},{1,9},{2,10},{3,11},{4,12},{5,13},{6,14},{7,15},{8,0},{9,1},... | collective-permute-start | bytes 6291464 | tf_op jit(solution)/shard_map/ppermute | solution.py:392
  176.4 48.6 %collective-permute-start.26 = (f32[512,512]{1,0:T(8,128)S(1)}, f32[512,512]{1,0:T(8,128)S(1)}, u32[]{:S(2)}, u32[]{:S(2)}) collective-permute-start(f32[512,512]{1,0:T(8,128)S(1)} %get-tuple-element.122), channel_id=1, source_target_pairs={{0,96},{16,112},{32,0},{48,16},{64,32},{80,48},{96,64},{112,80},{1... | collective-permute-start | bytes 3145736 | tf_op jit(solution)/shard_map/ppermute | solution.py:394
  178.4 46.6 %collective-permute-start.25 = (f32[512,512]{1,0:T(8,128)S(1)}, f32[512,512]{1,0:T(8,128)S(1)}, u32[]{:S(2)}, u32[]{:S(2)}) collective-permute-start(f32[512,512]{1,0:T(8,128)S(1)} %get-tuple-element.110), channel_id=1, source_target_pairs={{0,32},{16,48},{32,64},{48,80},{64,96},{80,112},{96,0},{112,16},{1... | collective-permute-start | bytes 3145736 | tf_op jit(solution)/shard_map/ppermute | solution.py:393
  178.4 46.1 %collective-permute-start.27 = (f32[256,512]{1,0:T(8,128)S(1)}, f32[256,512]{1,0:T(8,128)S(1)}, u32[]{:S(2)}, u32[]{:S(2)}) collective-permute-start(f32[256,512]{1,0:T(8,128)S(1)} %get-tuple-element.123), channel_id=1, source_target_pairs={{0,16},{16,0},{32,48},{48,32},{64,80},{80,64},{96,112},{112,96},{1... | collective-permute-start | bytes 1572872 | tf_op jit(solution)/shard_map/ppermute | solution.py:423
  202.3 29.4 %collective-permute-start.29 = (f32[256,512]{1,0:T(8,128)S(1)}, f32[256,512]{1,0:T(8,128)S(1)}, u32[]{:S(2)}, u32[]{:S(2)}) collective-permute-start(f32[256,512]{1,0:T(8,128)S(1)} %get-tuple-element.128), channel_id=1, source_target_pairs={{0,96},{16,112},{32,0},{48,16},{64,32},{80,48},{96,64},{112,80},{1... | collective-permute-start | bytes 1572872 | tf_op jit(solution)/shard_map/ppermute | solution.py:394
  221.4 12.6 %collective-permute-start.28 = (f32[256,512]{1,0:T(8,128)S(1)}, f32[256,512]{1,0:T(8,128)S(1)}, u32[]{:S(2)}, u32[]{:S(2)}) collective-permute-start(f32[256,512]{1,0:T(8,128)S(1)} %get-tuple-element.116), channel_id=1, source_target_pairs={{0,32},{16,48},{32,64},{48,80},{64,96},{80,112},{96,0},{112,16},{1... | collective-permute-start | bytes 1572872 | tf_op jit(solution)/shard_map/ppermute | solution.py:393
  224.5 21.9 %collective-permute-start.30 = (f32[256,512]{1,0:T(8,128)S(1)}, f32[256,512]{1,0:T(8,128)S(1)}, u32[]{:S(2)}, u32[]{:S(2)}) collective-permute-start(f32[256,512]{1,0:T(8,128)S(1)} %get-tuple-element.120), channel_id=1, source_target_pairs={{0,32},{16,48},{32,64},{48,80},{64,96},{80,112},{96,0},{112,16},{1... | collective-permute-start | bytes 1572872 | tf_op jit(solution)/shard_map/ppermute | solution.py:393
  229.3 17.2 %collective-permute-start.31 = (f32[256,512]{1,0:T(8,128)S(1)}, f32[256,512]{1,0:T(8,128)S(1)}, u32[]{:S(2)}, u32[]{:S(2)}) collective-permute-start(f32[256,512]{1,0:T(8,128)S(1)} %get-tuple-element.131), channel_id=1, source_target_pairs={{0,96},{16,112},{32,0},{48,16},{64,32},{80,48},{96,64},{112,80},{1... | collective-permute-start | bytes 1572872 | tf_op jit(solution)/shard_map/ppermute | solution.py:394
  238.8 25.5 %collective-permute-start.35 = (f32[512,512]{1,0:T(8,128)S(1)}, f32[512,512]{1,0:T(8,128)S(1)}, u32[]{:S(2)}, u32[]{:S(2)}) collective-permute-start(f32[512,512]{1,0:T(8,128)S(1)} %get-tuple-element.135), channel_id=1, source_target_pairs={{0,96},{16,112},{32,0},{48,16},{64,32},{80,48},{96,64},{112,80},{1... | collective-permute-start | bytes 3145736 | tf_op jit(solution)/shard_map/ppermute | solution.py:394
  242.6 26.5 %collective-permute-start.34 = (f32[512,512]{1,0:T(8,128)S(1)}, f32[512,512]{1,0:T(8,128)S(1)}, u32[]{:S(2)}, u32[]{:S(2)}) collective-permute-start(f32[512,512]{1,0:T(8,128)S(1)} %get-tuple-element.129), channel_id=1, source_target_pairs={{0,32},{16,48},{32,64},{48,80},{64,96},{80,112},{96,0},{112,16},{1... | collective-permute-start | bytes 3145736 | tf_op jit(solution)/shard_map/ppermute | solution.py:393
  242.6 11.5 %collective-permute-start.36 = (f32[256,512]{1,0:T(8,128)S(1)}, f32[256,512]{1,0:T(8,128)S(1)}, u32[]{:S(2)}, u32[]{:S(2)}) collective-permute-start(f32[256,512]{1,0:T(8,128)S(1)} %get-tuple-element.136), channel_id=1, source_target_pairs={{0,16},{16,0},{32,48},{48,32},{64,80},{80,64},{96,112},{112,96},{1... | collective-permute-start | bytes 1572872 | tf_op jit(solution)/shard_map/ppermute | solution.py:423
  251.2 35.5 %collective-permute-start.33 = (f32[512,512]{1,0:T(8,128)S(1)}, f32[512,512]{1,0:T(8,128)S(1)}, u32[]{:S(2)}, u32[]{:S(2)}) collective-permute-start(f32[512,512]{1,0:T(8,128)S(1)} %get-tuple-element.133), channel_id=1, source_target_pairs={{0,96},{16,112},{32,0},{48,16},{64,32},{80,48},{96,64},{112,80},{1... | collective-permute-start | bytes 3145736 | tf_op jit(solution)/shard_map/ppermute | solution.py:394
  254.1 37.5 %collective-permute-start.32 = (f32[512,512]{1,0:T(8,128)S(1)}, f32[512,512]{1,0:T(8,128)S(1)}, u32[]{:S(2)}, u32[]{:S(2)}) collective-permute-start(f32[512,512]{1,0:T(8,128)S(1)} %get-tuple-element.132), channel_id=1, source_target_pairs={{0,32},{16,48},{32,64},{48,80},{64,96},{80,112},{96,0},{112,16},{1... | collective-permute-start | bytes 3145736 | tf_op jit(solution)/shard_map/ppermute | solution.py:393
  273.3 18.2 %collective-permute-start.37 = (f32[256,512]{1,0:T(8,128)S(1)}, f32[256,512]{1,0:T(8,128)S(1)}, u32[]{:S(2)}, u32[]{:S(2)}) collective-permute-start(f32[256,512]{1,0:T(8,128)S(1)} %get-tuple-element.137), channel_id=1, source_target_pairs={{0,16},{16,0},{32,48},{48,32},{64,80},{80,64},{96,112},{112,96},{1... | collective-permute-start | bytes 1572872 | tf_op jit(solution)/shard_map/ppermute | solution.py:423
  295.8 3.2 %collective-permute-start.38 = (f32[256,512]{1,0:T(8,128)S(1)}, f32[256,512]{1,0:T(8,128)S(1)}, u32[]{:S(2)}, u32[]{:S(2)}) collective-permute-start(f32[256,512]{1,0:T(8,128)S(1)} %get-tuple-element.139), channel_id=1, source_target_pairs={{0,16},{16,0},{32,48},{48,32},{64,80},{80,64},{96,112},{112,96},{1... | collective-permute-start | bytes 1572872 | tf_op jit(solution)/shard_map/ppermute | solution.py:423

commit v3 on v2

--- a/solution.py
+++ b/solution.py
@@ -52,7 +52,7 @@
 
 
 SMALL = pl.CostEstimate(flops=0, bytes_accessed=1024, transcendentals=0)
-BIG_MIB, SMALL_MIB = 24, 24
+BIG_MIB, SMALL_MIB = 20, 20
 
 
 def call(body, grid, table, args, in_specs, out_shape, out_specs, name, mib=BIG_MIB, **more):

time: 301 us -> 301 us (level)
  no operation moved by 1% of the time
where the time goes in v3:
time: 301 us
  waiting for transfers between devices  117 us (39%)
  starting transfers between devices  68.8 us (23%)
  Pallas kernels  56.1 us (19%)
  blocking collectives  53.6 us (18%)
  local copies, waits for them, and re-layouts  4.5 us (1%)
    pallas_call x20, Pallas kernels, call(): pl.pallas_call(body, out_shape=out_shape, grid_spec=pltpu.PrefetchScalarG...  56.1 us
    all_to_all x1, blocking collectives, per_device(): own = lax.all_to_all(chosen, 'col', split_axis=0, concat_axis=0, tiled=True)  53.6 us
    ppermute x8, waiting for transfers between devices, per_device(): down_z = lambda v: lax.ppermute(v, 'row', z_shift(-1))  34.3 us
    ppermute x3, waiting for transfers between devices, per_device(): lax.ppermute(array, ANYWHERE, plane_shift(False, t))  25.6 us
    ppermute x12, waiting for transfers between devices, per_device(): lax.ppermute(a, ANYWHERE, plane_shift(True, s))  21.4 us
    ppermute x4, starting transfers between devices, here(): return (result, (lax.ppermute(theirs, 'row', OTHER_CORE), at[f'theirs{t}']))  20.2 us
    ppermute x8, starting transfers between devices, per_device(): down_z = lambda v: lax.ppermute(v, 'row', z_shift(-1))  18.2 us
    ppermute x3, waiting for transfers between devices, per_device(): lax.ppermute(amplitudes, 'row', z_shift(k))  15.8 us
  transfers between devices with their start and end apart: 39, of which 19 were waited for; matrix products, arithmetic and copies ran while one was open for 0% of the time, Pallas kernels for 16%

profile of v3, /device:TPU:3, one launch (start us, length us, event | category | flops | bytes accessed | tf_op | source)
XLA Modules:
  0.0 300.6 jit_solution(11362393738800405247)
XLA Ops:
  1.4 3.4 %copy-done = f32[128,1,1,128,128]{4,3,2,1,0:T(8,128)S(1)} copy-done((f32[128,1,1,128,128]{4,3,2,1,0:T(8,128)S(1)}, f32[128,1,1,128,128]{4,3,2,1,0:T(8,128)}, u32[]{:S(2)}) %copy-start) | copy-done | bytes 8388632
  4.7 1.0 pick_tiles.3
  5.8 1.4 collective-permute-start
  7.1 2.6 collective-permute-start.1
  9.8 1.1 collective-permute-start.2
  10.8 3.6 %collective-permute-start.4 = (f32[128,1024]{1,0:T(8,128)S(1)}, f32[128,1024]{1,0:T(8,128)S(1)}, u32[]{:S(2)}, u32[]{:S(2)}) collective-permute-start(f32[128,1024]{1,0:T(8,128)S(1)} %copy-done.1), channel_id=1, source_target_pairs={{0,64},{16,80},{32,96},{48,112},{64,0},{80,16},{96,32},{112,48},{1... | collective-permute-start | bytes 1572872 | tf_op jit(solution)/shard_map/ppermute | solution.py:397
  15.3 3.8 %collective-permute-start.5 = (f32[128,1024]{1,0:T(8,128)S(1)}, f32[128,1024]{1,0:T(8,128)S(1)}, u32[]{:S(2)}, u32[]{:S(2)}) collective-permute-start(f32[128,1024]{1,0:T(8,128)S(1)} %copy-done.1), channel_id=1, source_target_pairs={{0,96},{16,112},{32,0},{48,16},{64,32},{80,48},{96,64},{112,80},{1... | collective-permute-start | bytes 1572872 | tf_op jit(solution)/shard_map/ppermute | solution.py:397
  19.0 3.2 %collective-permute-done.1.refs_4_ = f32[1,8,128,128]{3,2,1,0:T(8,128)S(1)} collective-permute-done((f32[1,8,128,128]{3,2,1,0:T(8,128)S(1)}, f32[1,8,128,128]{3,2,1,0:T(8,128)S(1)}, u32[]{:S(2)}, u32[]{:S(2)}) %collective-permute-start.1) | collective-permute-done | bytes 524320 | tf_op jit(solution)/shard_map/ppermute | solution.py:390
  22.2 4.1 %collective-permute-done.4.refs_2_ = f32[128,1024]{1,0:T(8,128)S(1)} collective-permute-done((f32[128,1024]{1,0:T(8,128)S(1)}, f32[128,1024]{1,0:T(8,128)S(1)}, u32[]{:S(2)}, u32[]{:S(2)}) %collective-permute-start.4) | collective-permute-done | bytes 524320 | tf_op jit(solution)/shard_map/ppermute | solution.py:397
  26.4 11.7 %collective-permute-done.3.refs_1_ = f32[128,1024]{1,0:T(8,128)S(1)} collective-permute-done((f32[128,1024]{1,0:T(8,128)S(1)}, f32[128,1024]{1,0:T(8,128)S(1)}, u32[]{:S(2)}, u32[]{:S(2)}) %collective-permute-start.3) | collective-permute-done | bytes 524320 | tf_op jit(solution)/shard_map/ppermute | solution.py:397
  38.0 1.4 choose.1
  39.4 53.6 %all_to_all.5 = f32[16,128,512]{2,1,0:T(8,128)S(1)} all-to-all(f32[16,128,512]{2,1,0:T(8,128)S(1)} %choose.1), channel_id=1, replica_groups=mesh['row'=8,'col'=16] {'col'}, dimensions={0} | all-to-all | bytes 8388608 | tf_op jit(solution)/shard_map/all_to_all | solution.py:402
  93.0 2.0 collective-permute-start.6
  95.0 0.9 pick_tiles.4
  96.0 1.7 collective-permute-start.8
  97.8 0.9 collective-permute-start.9
  98.7 3.1 %collective-permute-done.6.refs_1_ = f32[2048,512]{1,0:T(8,128)S(1)} collective-permute-done((f32[2048,512]{1,0:T(8,128)S(1)}, f32[2048,512]{1,0:T(8,128)S(1)}, u32[]{:S(2)}, u32[]{:S(2)}) %collective-permute-start.6) | collective-permute-done | bytes 4194336 | tf_op jit(solution)/shard_map/ppermute | solution.py:404
  101.8 3.1 %products_away.4 = (f32[256,512]{1,0:T(8,128)S(1)}, f32[256,512]{1,0:T(8,128)S(1)}, bf16[1024,512]{1,0:T(8,128)(2,1)S(1)}, bf16[1024,512]{1,0:T(8,128)(2,1)S(1)}) custom-call(s32[193]{0:T(256)S(1)} %concatenate.3.table_ref, f32[2048,512]{1,0:T(8,128)S(1)} %bitcast.86, f32[2048,512]{1,0:T(8,128)S(1)} %collective-permute-done.6.refs_1_, ...), custom_call_target="tpu_custom_call" | custom-call | bytes 1024 | tf_op jit(solution)/shard_map/products_away/pallas_call | solution.py:60
  104.9 1.3 pick_tiles.5
  106.2 4.7 %collective-permute-done.7.refs_0_ = f32[1,8,128,128]{3,2,1,0:T(8,128)S(1)} collective-permute-done((f32[1,8,128,128]{3,2,1,0:T(8,128)S(1)}, f32[1,8,128,128]{3,2,1,0:T(8,128)S(1)}, u32[]{:S(2)}, u32[]{:S(2)}) %collective-permute-start.7) | collective-permute-done | bytes 524320 | tf_op jit(solution)/shard_map/ppermute | solution.py:390
  110.9 0.9 collective-permute-done.9.refs_2_
  111.8 0.9 join_tiles.3
  112.7 2.5 collective-permute-start.11
  115.7 9.5 %collective-permute-done.11.refs_5_ = f32[256,512]{1,0:T(8,128)S(1)} collective-permute-done((f32[256,512]{1,0:T(8,128)S(1)}, f32[256,512]{1,0:T(8,128)S(1)}, u32[]{:S(2)}, u32[]{:S(2)}) %collective-permute-start.11) | collective-permute-done | bytes 524320 | tf_op jit(solution)/shard_map/ppermute | solution.py:394
  125.2 3.1 %collective-permute-done.10.refs_4_ = f32[256,512]{1,0:T(8,128)S(1)} collective-permute-done((f32[256,512]{1,0:T(8,128)S(1)}, f32[256,512]{1,0:T(8,128)S(1)}, u32[]{:S(2)}, u32[]{:S(2)}) %collective-permute-start.10) | collective-permute-done | bytes 524320 | tf_op jit(solution)/shard_map/ppermute | solution.py:393
  128.3 4.8 %products_next.4 = (f32[512,512]{1,0:T(8,128)S(1)}, f32[512,512]{1,0:T(8,128)S(1)}) custom-call(s32[193]{0:T(256)S(1)} %concatenate.3.table_ref, f32[2048,512]{1,0:T(8,128)S(1)} %bitcast.87, f32[2048,512]{1,0:T(8,128)S(1)} %collective-permute-done.6.refs_1_, bf16[1024,512]{1,0:T(8,128)(2,1)S(1)} %get-tuple-element.93.refs_2_, ...), custom_call_target="tpu_custom_call" | custom-call | bytes 1024 | tf_op jit(solution)/shard_map/products_next/pallas_call | solution.py:60
  133.4 1.2 collective-permute-start.16
  135.1 2.2 collective-permute-start.14
  137.3 12.5 %collective-permute-done.13.refs_1_ = f32[1,8,128,128]{3,2,1,0:T(8,128)S(1)} collective-permute-done((f32[1,8,128,128]{3,2,1,0:T(8,128)S(1)}, f32[1,8,128,128]{3,2,1,0:T(8,128)S(1)}, u32[]{:S(2)}, u32[]{:S(2)}) %collective-permute-start.13) | collective-permute-done | bytes 524320 | tf_op jit(solution)/shard_map/ppermute | solution.py:390
  149.8 0.9 join_tiles.4
  150.7 3.1 %products_away.5 = (f32[256,512]{1,0:T(8,128)S(1)}, f32[256,512]{1,0:T(8,128)S(1)}, bf16[1024,512]{1,0:T(8,128)(2,1)S(1)}, bf16[1024,512]{1,0:T(8,128)(2,1)S(1)}) custom-call(s32[193]{0:T(256)S(1)} %concatenate.3.table_ref, f32[2048,512]{1,0:T(8,128)S(1)} %bitcast.88, f32[2048,512]{1,0:T(8,128)S(1)} %collective-permute-done.6.refs_1_, ...), custom_call_target="tpu_custom_call" | custom-call | bytes 1024 | tf_op jit(solution)/shard_map/products_away/pallas_call | solution.py:60
  153.8 1.7 collective-permute-start.19
  156.1 2.4 collective-permute-start.21
  158.8 3.4 %products_here.4 = (f32[256,512]{1,0:T(8,128)S(1)}, f32[256,4096]{1,0:T(8,128)}) custom-call(s32[193]{0:T(256)S(1)} %concatenate.3.table_ref, f32[2048,512]{1,0:T(8,128)S(1)} %bitcast.89, f32[2048,512]{1,0:T(8,128)S(1)} %collective-permute-done.6.refs_1_, bf16[1024,512]{1,0:T(8,128)(2,1)S(1)} %get-tuple-element.93.refs_2_, ...), custom_call_target="tpu_custom_call" | custom-call | bytes 1024 | tf_op jit(solution)/shard_map/products_here/pallas_call | solution.py:60
  162.2 4.2 %collective-permute-done.19.refs_5_ = f32[256,512]{1,0:T(8,128)S(1)} collective-permute-done((f32[256,512]{1,0:T(8,128)S(1)}, f32[256,512]{1,0:T(8,128)S(1)}, u32[]{:S(2)}, u32[]{:S(2)}) %collective-permute-start.19) | collective-permute-done | bytes 524320 | tf_op jit(solution)/shard_map/ppermute | solution.py:394
  166.4 2.0 collective-permute-start.23
  168.5 4.8 %products_next.5 = (f32[512,512]{1,0:T(8,128)S(1)}, f32[512,512]{1,0:T(8,128)S(1)}) custom-call(s32[193]{0:T(256)S(1)} %concatenate.3.table_ref, f32[2048,512]{1,0:T(8,128)S(1)} %bitcast.90, f32[2048,512]{1,0:T(8,128)S(1)} %collective-permute-done.6.refs_1_, bf16[1024,512]{1,0:T(8,128)(2,1)S(1)} %get-tuple-element.107.refs_2_, ...), custom_call_target="tpu_custom_call" | custom-call | bytes 1024 | tf_op jit(solution)/shard_map/products_next/pallas_call | solution.py:60
  173.3 0.9 join_tiles.5
  174.1 2.2 collective-permute-start.24
  176.4 2.0 collective-permute-start.26
  178.4 11.9 %collective-permute-start.27 = (f32[256,512]{1,0:T(8,128)S(1)}, f32[256,512]{1,0:T(8,128)S(1)}, u32[]{:S(2)}, u32[]{:S(2)}) collective-permute-start(f32[256,512]{1,0:T(8,128)S(1)} %get-tuple-element.123), channel_id=1, source_target_pairs={{0,16},{16,0},{32,48},{48,32},{64,80},{80,64},{96,112},{112,96},{1... | collective-permute-start | bytes 1572872 | tf_op jit(solution)/shard_map/ppermute | solution.py:423
  190.2 9.0 %collective-permute-done.23.refs_2_ = f32[4,8,128,128]{3,2,1,0:T(8,128)S(1)} collective-permute-done((f32[4,8,128,128]{3,2,1,0:T(8,128)S(1)}, f32[4,8,128,128]{3,2,1,0:T(8,128)S(1)}, u32[]{:S(2)}, u32[]{:S(2)}) %collective-permute-start.23) | collective-permute-done | bytes 2097184 | tf_op jit(solution)/shard_map/ppermute | solution.py:392
  199.2 3.1 %products_away.6 = (f32[256,512]{1,0:T(8,128)S(1)}, f32[256,512]{1,0:T(8,128)S(1)}, bf16[1024,512]{1,0:T(8,128)(2,1)S(1)}, bf16[1024,512]{1,0:T(8,128)(2,1)S(1)}) custom-call(s32[193]{0:T(256)S(1)} %concatenate.3.table_ref, f32[2048,512]{1,0:T(8,128)S(1)} %bitcast.91, f32[2048,512]{1,0:T(8,128)S(1)} %collective-permute-done.6.refs_1_, ...), custom_call_target="tpu_custom_call" | custom-call | bytes 1024 | tf_op jit(solution)/shard_map/products_away/pallas_call | solution.py:60
  202.3 2.5 collective-permute-start.29
  204.8 16.6 %collective-permute-done.24.refs_2_ = f32[4,8,128,128]{3,2,1,0:T(8,128)S(1)} collective-permute-done((f32[4,8,128,128]{3,2,1,0:T(8,128)S(1)}, f32[4,8,128,128]{3,2,1,0:T(8,128)S(1)}, u32[]{:S(2)}, u32[]{:S(2)}) %collective-permute-start.24) | collective-permute-done | bytes 2097184 | tf_op jit(solution)/shard_map/ppermute | solution.py:392
  221.4 3.1 %products_away.7 = (f32[256,512]{1,0:T(8,128)S(1)}, f32[256,512]{1,0:T(8,128)S(1)}, bf16[1024,512]{1,0:T(8,128)(2,1)S(1)}, bf16[1024,512]{1,0:T(8,128)(2,1)S(1)}) custom-call(s32[193]{0:T(256)S(1)} %concatenate.3.table_ref, f32[2048,512]{1,0:T(8,128)S(1)} %bitcast.92, f32[2048,512]{1,0:T(8,128)S(1)} %collective-permute-done.6.refs_1_, ...), custom_call_target="tpu_custom_call" | custom-call | bytes 1024 | tf_op jit(solution)/shard_map/products_away/pallas_call | solution.py:60
  225.0 4.3 %products_here.5 = (f32[256,512]{1,0:T(8,128)S(1)}, f32[256,4096]{1,0:T(8,128)}) custom-call(s32[193]{0:T(256)S(1)} %concatenate.3.table_ref, f32[2048,512]{1,0:T(8,128)S(1)} %bitcast.93, f32[2048,512]{1,0:T(8,128)S(1)} %collective-permute-done.6.refs_1_, bf16[1024,512]{1,0:T(8,128)(2,1)S(1)} %get-tuple-element.107.refs_2_, ...), custom_call_target="tpu_custom_call", output_to_operand_aliasing={{1}: (8, {})} | custom-call | bytes 1024 | tf_op jit(solution)/shard_map/products_here/pallas_call | solution.py:60
  229.3 2.4 collective-permute-start.31
  231.7 2.3 collective-permute-done.28.refs_4_
  234.0 4.8 %products_next.6 = (f32[512,512]{1,0:T(8,128)S(1)}, f32[512,512]{1,0:T(8,128)S(1)}) custom-call(s32[193]{0:T(256)S(1)} %concatenate.3.table_ref, f32[2048,512]{1,0:T(8,128)S(1)} %bitcast.94, f32[2048,512]{1,0:T(8,128)S(1)} %collective-permute-done.6.refs_1_, bf16[1024,512]{1,0:T(8,128)(2,1)S(1)} %get-tuple-element.126.refs_2_, ...), custom_call_target="tpu_custom_call" | custom-call | bytes 1024 | tf_op jit(solution)/shard_map/products_next/pallas_call | solution.py:60
  238.8 3.9 %collective-permute-start.35 = (f32[512,512]{1,0:T(8,128)S(1)}, f32[512,512]{1,0:T(8,128)S(1)}, u32[]{:S(2)}, u32[]{:S(2)}) collective-permute-start(f32[512,512]{1,0:T(8,128)S(1)} %get-tuple-element.135), channel_id=1, source_target_pairs={{0,96},{16,112},{32,0},{48,16},{64,32},{80,48},{96,64},{112,80},{1... | collective-permute-start | bytes 3145736 | tf_op jit(solution)/shard_map/ppermute | solution.py:394
  242.6 3.8 %collective-permute-start.36 = (f32[256,512]{1,0:T(8,128)S(1)}, f32[256,512]{1,0:T(8,128)S(1)}, u32[]{:S(2)}, u32[]{:S(2)}) collective-permute-start(f32[256,512]{1,0:T(8,128)S(1)} %get-tuple-element.136), channel_id=1, source_target_pairs={{0,16},{16,0},{32,48},{48,32},{64,80},{80,64},{96,112},{112,96},{1... | collective-permute-start | bytes 1572872 | tf_op jit(solution)/shard_map/ppermute | solution.py:423
  246.4 4.8 %products_next.7 = (f32[512,512]{1,0:T(8,128)S(1)}, f32[512,512]{1,0:T(8,128)S(1)}) custom-call(s32[193]{0:T(256)S(1)} %concatenate.3.table_ref, f32[2048,512]{1,0:T(8,128)S(1)} %bitcast.95, f32[2048,512]{1,0:T(8,128)S(1)} %collective-permute-done.6.refs_1_, bf16[1024,512]{1,0:T(8,128)(2,1)S(1)} %get-tuple-element.118.refs_2_, ...), custom_call_target="tpu_custom_call" | custom-call | bytes 1024 | tf_op jit(solution)/shard_map/products_next/pallas_call | solution.py:60
  251.2 2.9 collective-permute-start.33
  254.1 10.2 %collective-permute-done.35.refs_5_ = f32[512,512]{1,0:T(8,128)S(1)} collective-permute-done((f32[512,512]{1,0:T(8,128)S(1)}, f32[512,512]{1,0:T(8,128)S(1)}, u32[]{:S(2)}, u32[]{:S(2)}) %collective-permute-start.35) | collective-permute-done | bytes 1048608 | tf_op jit(solution)/shard_map/ppermute | solution.py:394
  264.3 4.8 %collective-permute-done.34.refs_4_ = f32[512,512]{1,0:T(8,128)S(1)} collective-permute-done((f32[512,512]{1,0:T(8,128)S(1)}, f32[512,512]{1,0:T(8,128)S(1)}, u32[]{:S(2)}, u32[]{:S(2)}) %collective-permute-start.34) | collective-permute-done | bytes 1048608 | tf_op jit(solution)/shard_map/ppermute | solution.py:393
  269.1 4.3 %products_here.6 = (f32[256,512]{1,0:T(8,128)S(1)}, f32[256,4096]{1,0:T(8,128)}) custom-call(s32[193]{0:T(256)S(1)} %concatenate.3.table_ref, f32[2048,512]{1,0:T(8,128)S(1)} %bitcast.96, f32[2048,512]{1,0:T(8,128)S(1)} %collective-permute-done.6.refs_1_, bf16[1024,512]{1,0:T(8,128)(2,1)S(1)} %get-tuple-element.126.refs_2_, ...), custom_call_target="tpu_custom_call", output_to_operand_aliasing={{1}: (8, {})} | custom-call | bytes 1024 | tf_op jit(solution)/shard_map/products_here/pallas_call | solution.py:60
  273.3 2.9 collective-permute-start.37
  276.2 10.5 %collective-permute-done.33.refs_5_ = f32[512,512]{1,0:T(8,128)S(1)} collective-permute-done((f32[512,512]{1,0:T(8,128)S(1)}, f32[512,512]{1,0:T(8,128)S(1)}, u32[]{:S(2)}, u32[]{:S(2)}) %collective-permute-start.33) | collective-permute-done | bytes 1048608 | tf_op jit(solution)/shard_map/ppermute | solution.py:394
  286.7 4.8 %collective-permute-done.32.refs_4_ = f32[512,512]{1,0:T(8,128)S(1)} collective-permute-done((f32[512,512]{1,0:T(8,128)S(1)}, f32[512,512]{1,0:T(8,128)S(1)}, u32[]{:S(2)}, u32[]{:S(2)}) %collective-permute-start.32) | collective-permute-done | bytes 1048608 | tf_op jit(solution)/shard_map/ppermute | solution.py:393
  291.6 4.3 %products_here.7 = (f32[256,512]{1,0:T(8,128)S(1)}, f32[256,4096]{1,0:T(8,128)}) custom-call(s32[193]{0:T(256)S(1)} %concatenate.3.table_ref, f32[2048,512]{1,0:T(8,128)S(1)} %bitcast.97, f32[2048,512]{1,0:T(8,128)S(1)} %collective-permute-done.6.refs_1_, bf16[1024,512]{1,0:T(8,128)(2,1)S(1)} %get-tuple-element.118.refs_2_, ...), custom_call_target="tpu_custom_call", output_to_operand_aliasing={{1}: (8, {})} | custom-call | bytes 1024 | tf_op jit(solution)/shard_map/products_here/pallas_call | solution.py:60
  295.8 1.7 collective-permute-start.38
  297.5 1.5 collective-permute-done.38.theirs_ref
  299.1 1.4 place.1
  (53 shorter events, 4.9 us)
Async XLA Ops:
  1.4 3.4 %copy-start = (f32[128,1,1,128,128]{4,3,2,1,0:T(8,128)S(1)}, f32[128,1,1,128,128]{4,3,2,1,0:T(8,128)}, u32[]{:S(2)}) copy-start(f32[128,1,1,128,128]{4,3,2,1,0:T(8,128)} %param.4) | copy-start | bytes 25165828
  4.7 6.1 %copy-start.1 = (f32[128,1024]{1,0:T(8,128)S(1)}, f32[128,1024]{1,0:T(8,128)}, u32[]{:S(2)}) copy-start(f32[128,1024]{1,0:T(8,128)} %refs_0_.1) | copy-start | bytes 1572868
  4.7 90.3 %slice-start = ((s8[8388608]{0:T(1024)(128)(4,1)}), s8[4194304]{0:T(1024)(128)(4,1)S(1)}, s32[]{:S(2)}) async-start(s8[8388608]{0:T(1024)(128)(4,1)} %bitcast.99), calls=%async_computation.1 | async-start | bytes 8388608
  5.8 9.5 %collective-permute-start = (f32[1,8,128,128]{3,2,1,0:T(8,128)S(1)}, f32[1,8,128,128]{3,2,1,0:T(8,128)S(1)}, u32[]{:S(2)}, u32[]{:S(2)}) collective-permute-start(f32[1,8,128,128]{3,2,1,0:T(8,128)S(1)} %get-tuple-element.74), channel_id=1, source_target_pairs={{0,1},{1,2},{2,3},{3,0},{4,5},{5,6},{6,7},{7,4},{8,9},{9,10},{10,1... | collective-permute-start | bytes 1572872 | tf_op jit(solution)/shard_map/ppermute | solution.py:390
  7.1 15.1 %collective-permute-start.1 = (f32[1,8,128,128]{3,2,1,0:T(8,128)S(1)}, f32[1,8,128,128]{3,2,1,0:T(8,128)S(1)}, u32[]{:S(2)}, u32[]{:S(2)}) collective-permute-start(f32[1,8,128,128]{3,2,1,0:T(8,128)S(1)} %get-tuple-element.75), channel_id=1, source_target_pairs={{0,2},{1,3},{2,0},{3,1},{4,6},{5,7},{6,4},{7,5},{8,10},{9,11},{10,... | collective-permute-start | bytes 1572872 | tf_op jit(solution)/shard_map/ppermute | solution.py:390
  9.8 12.5 %collective-permute-start.2 = (f32[1,8,128,128]{3,2,1,0:T(8,128)S(1)}, f32[1,8,128,128]{3,2,1,0:T(8,128)S(1)}, u32[]{:S(2)}, u32[]{:S(2)}) collective-permute-start(f32[1,8,128,128]{3,2,1,0:T(8,128)S(1)} %get-tuple-element.76), channel_id=1, source_target_pairs={{0,3},{1,0},{2,1},{3,2},{4,7},{5,4},{6,5},{7,6},{8,11},{9,8},{10,9... | collective-permute-start | bytes 1572872 | tf_op jit(solution)/shard_map/ppermute | solution.py:390
  10.8 15.5 %collective-permute-start.4 = (f32[128,1024]{1,0:T(8,128)S(1)}, f32[128,1024]{1,0:T(8,128)S(1)}, u32[]{:S(2)}, u32[]{:S(2)}) collective-permute-start(f32[128,1024]{1,0:T(8,128)S(1)} %copy-done.1), channel_id=1, source_target_pairs={{0,64},{16,80},{32,96},{48,112},{64,0},{80,16},{96,32},{112,48},{1... | collective-permute-start | bytes 1572872 | tf_op jit(solution)/shard_map/ppermute | solution.py:397
  14.4 23.6 %collective-permute-start.3 = (f32[128,1024]{1,0:T(8,128)S(1)}, f32[128,1024]{1,0:T(8,128)S(1)}, u32[]{:S(2)}, u32[]{:S(2)}) collective-permute-start(f32[128,1024]{1,0:T(8,128)S(1)} %copy-done.1), channel_id=1, source_target_pairs={{0,32},{16,48},{32,64},{48,80},{64,96},{80,112},{96,0},{112,16},{1... | collective-permute-start | bytes 1572872 | tf_op jit(solution)/shard_map/ppermute | solution.py:397
  15.3 22.8 %collective-permute-start.5 = (f32[128,1024]{1,0:T(8,128)S(1)}, f32[128,1024]{1,0:T(8,128)S(1)}, u32[]{:S(2)}, u32[]{:S(2)}) collective-permute-start(f32[128,1024]{1,0:T(8,128)S(1)} %copy-done.1), channel_id=1, source_target_pairs={{0,96},{16,112},{32,0},{48,16},{64,32},{80,48},{96,64},{112,80},{1... | collective-permute-start | bytes 1572872 | tf_op jit(solution)/shard_map/ppermute | solution.py:397
  22.2 72.8 %slice-start.1 = ((s8[8388608]{0:T(1024)(128)(4,1)}), s8[4194304]{0:T(1024)(128)(4,1)S(1)}, s32[]{:S(2)}) async-start(s8[8388608]{0:T(1024)(128)(4,1)} %bitcast.99), calls=%async_computation.2 | async-start | bytes 8388608
  93.0 8.8 %collective-permute-start.6 = (f32[2048,512]{1,0:T(8,128)S(1)}, f32[2048,512]{1,0:T(8,128)S(1)}, u32[]{:S(2)}, u32[]{:S(2)}) collective-permute-start(f32[2048,512]{1,0:T(8,128)S(1)} %bitcast.85), channel_id=1, source_target_pairs={{0,16},{16,0},{32,48},{48,32},{64,80},{80,64},{96,112},{112,96},{1... | collective-permute-start | bytes 12582920 | tf_op jit(solution)/shard_map/ppermute | solution.py:404
  95.9 14.9 %collective-permute-start.7 = (f32[1,8,128,128]{3,2,1,0:T(8,128)S(1)}, f32[1,8,128,128]{3,2,1,0:T(8,128)S(1)}, u32[]{:S(2)}, u32[]{:S(2)}) collective-permute-start(f32[1,8,128,128]{3,2,1,0:T(8,128)S(1)} %get-tuple-element.79), channel_id=1, source_target_pairs={{0,1},{1,2},{2,3},{3,0},{4,5},{5,6},{6,7},{7,4},{8,9},{9,10},{10,1... | collective-permute-start | bytes 1572872 | tf_op jit(solution)/shard_map/ppermute | solution.py:390
  96.0 14.8 %collective-permute-start.8 = (f32[1,8,128,128]{3,2,1,0:T(8,128)S(1)}, f32[1,8,128,128]{3,2,1,0:T(8,128)S(1)}, u32[]{:S(2)}, u32[]{:S(2)}) collective-permute-start(f32[1,8,128,128]{3,2,1,0:T(8,128)S(1)} %get-tuple-element.80), channel_id=1, source_target_pairs={{0,2},{1,3},{2,0},{3,1},{4,6},{5,7},{6,4},{7,5},{8,10},{9,11},{10,... | collective-permute-start | bytes 1572872 | tf_op jit(solution)/shard_map/ppermute | solution.py:390
  97.8 14.0 %collective-permute-start.9 = (f32[1,8,128,128]{3,2,1,0:T(8,128)S(1)}, f32[1,8,128,128]{3,2,1,0:T(8,128)S(1)}, u32[]{:S(2)}, u32[]{:S(2)}) collective-permute-start(f32[1,8,128,128]{3,2,1,0:T(8,128)S(1)} %get-tuple-element.81), channel_id=1, source_target_pairs={{0,3},{1,0},{2,1},{3,2},{4,7},{5,4},{6,5},{7,6},{8,11},{9,8},{10,9... | collective-permute-start | bytes 1572872 | tf_op jit(solution)/shard_map/ppermute | solution.py:390
  112.7 38.1 %collective-permute-start.15 = (f32[4,8,128,128]{3,2,1,0:T(8,128)S(1)}, f32[4,8,128,128]{3,2,1,0:T(8,128)S(1)}, u32[]{:S(2)}, u32[]{:S(2)}) collective-permute-start(f32[4,8,128,128]{3,2,1,0:T(8,128)S(1)} %join_tiles.3), channel_id=1, source_target_pairs={{0,4},{1,5},{2,6},{3,7},{4,8},{5,9},{6,10},{7,11},{8,12},{9,13},{1... | collective-permute-start | bytes 6291464 | tf_op jit(solution)/shard_map/ppermute | solution.py:392
  112.7 12.4 %collective-permute-start.11 = (f32[256,512]{1,0:T(8,128)S(1)}, f32[256,512]{1,0:T(8,128)S(1)}, u32[]{:S(2)}, u32[]{:S(2)}) collective-permute-start(f32[256,512]{1,0:T(8,128)S(1)} %get-tuple-element.95), channel_id=1, source_target_pairs={{0,96},{16,112},{32,0},{48,16},{64,32},{80,48},{96,64},{112,80},{1... | collective-permute-start | bytes 1572872 | tf_op jit(solution)/shard_map/ppermute | solution.py:394
  115.3 13.1 %collective-permute-start.10 = (f32[256,512]{1,0:T(8,128)S(1)}, f32[256,512]{1,0:T(8,128)S(1)}, u32[]{:S(2)}, u32[]{:S(2)}) collective-permute-start(f32[256,512]{1,0:T(8,128)S(1)} %get-tuple-element.83), channel_id=1, source_target_pairs={{0,32},{16,48},{32,64},{48,80},{64,96},{80,112},{96,0},{112,16},{1... | collective-permute-start | bytes 1572872 | tf_op jit(solution)/shard_map/ppermute | solution.py:393
  115.3 19.9 %collective-permute-start.12 = (f32[1,8,128,128]{3,2,1,0:T(8,128)S(1)}, f32[1,8,128,128]{3,2,1,0:T(8,128)S(1)}, u32[]{:S(2)}, u32[]{:S(2)}) collective-permute-start(f32[1,8,128,128]{3,2,1,0:T(8,128)S(1)} %get-tuple-element.98), channel_id=1, source_target_pairs={{0,1},{1,2},{2,3},{3,0},{4,5},{5,6},{6,7},{7,4},{8,9},{9,10},{10,1... | collective-permute-start | bytes 1572872 | tf_op jit(solution)/shard_map/ppermute | solution.py:390
  133.1 23.0 %collective-permute-start.17 = (f32[512,512]{1,0:T(8,128)S(1)}, f32[512,512]{1,0:T(8,128)S(1)}, u32[]{:S(2)}, u32[]{:S(2)}) collective-permute-start(f32[512,512]{1,0:T(8,128)S(1)} %get-tuple-element.104), channel_id=1, source_target_pairs={{0,96},{16,112},{32,0},{48,16},{64,32},{80,48},{96,64},{112,80},{1... | collective-permute-start | bytes 3145736 | tf_op jit(solution)/shard_map/ppermute | solution.py:394
  133.4 25.0 %collective-permute-start.16 = (f32[512,512]{1,0:T(8,128)S(1)}, f32[512,512]{1,0:T(8,128)S(1)}, u32[]{:S(2)}, u32[]{:S(2)}) collective-permute-start(f32[512,512]{1,0:T(8,128)S(1)} %get-tuple-element.96), channel_id=1, source_target_pairs={{0,32},{16,48},{32,64},{48,80},{64,96},{80,112},{96,0},{112,16},{1... | collective-permute-start | bytes 3145736 | tf_op jit(solution)/shard_map/ppermute | solution.py:393
  134.6 15.2 %collective-permute-start.13 = (f32[1,8,128,128]{3,2,1,0:T(8,128)S(1)}, f32[1,8,128,128]{3,2,1,0:T(8,128)S(1)}, u32[]{:S(2)}, u32[]{:S(2)}) collective-permute-start(f32[1,8,128,128]{3,2,1,0:T(8,128)S(1)} %get-tuple-element.99), channel_id=1, source_target_pairs={{0,2},{1,3},{2,0},{3,1},{4,6},{5,7},{6,4},{7,5},{8,10},{9,11},{10,... | collective-permute-start | bytes 1572872 | tf_op jit(solution)/shard_map/ppermute | solution.py:390
  135.1 14.7 %collective-permute-start.14 = (f32[1,8,128,128]{3,2,1,0:T(8,128)S(1)}, f32[1,8,128,128]{3,2,1,0:T(8,128)S(1)}, u32[]{:S(2)}, u32[]{:S(2)}) collective-permute-start(f32[1,8,128,128]{3,2,1,0:T(8,128)S(1)} %get-tuple-element.100), channel_id=1, source_target_pairs={{0,3},{1,0},{2,1},{3,2},{4,7},{5,4},{6,5},{7,6},{8,11},{9,8},{10,9... | collective-permute-start | bytes 1572872 | tf_op jit(solution)/shard_map/ppermute | solution.py:390
  153.8 12.6 %collective-permute-start.19 = (f32[256,512]{1,0:T(8,128)S(1)}, f32[256,512]{1,0:T(8,128)S(1)}, u32[]{:S(2)}, u32[]{:S(2)}) collective-permute-start(f32[256,512]{1,0:T(8,128)S(1)} %get-tuple-element.109), channel_id=1, source_target_pairs={{0,96},{16,112},{32,0},{48,16},{64,32},{80,48},{96,64},{112,80},{1... | collective-permute-start | bytes 1572872 | tf_op jit(solution)/shard_map/ppermute | solution.py:394
  155.6 12.9 %collective-permute-start.18 = (f32[256,512]{1,0:T(8,128)S(1)}, f32[256,512]{1,0:T(8,128)S(1)}, u32[]{:S(2)}, u32[]{:S(2)}) collective-permute-start(f32[256,512]{1,0:T(8,128)S(1)} %get-tuple-element.102), channel_id=1, source_target_pairs={{0,32},{16,48},{32,64},{48,80},{64,96},{80,112},{96,0},{112,16},{1... | collective-permute-start | bytes 1572872 | tf_op jit(solution)/shard_map/ppermute | solution.py:393
  155.6 17.7 %collective-permute-start.20 = (f32[1,8,128,128]{3,2,1,0:T(8,128)S(1)}, f32[1,8,128,128]{3,2,1,0:T(8,128)S(1)}, u32[]{:S(2)}, u32[]{:S(2)}) collective-permute-start(f32[1,8,128,128]{3,2,1,0:T(8,128)S(1)} %get-tuple-element.112), channel_id=1, source_target_pairs={{0,1},{1,2},{2,3},{3,0},{4,5},{5,6},{6,7},{7,4},{8,9},{9,10},{10,1... | collective-permute-start | bytes 1572872 | tf_op jit(solution)/shard_map/ppermute | solution.py:390
  156.1 17.1 %collective-permute-start.21 = (f32[1,8,128,128]{3,2,1,0:T(8,128)S(1)}, f32[1,8,128,128]{3,2,1,0:T(8,128)S(1)}, u32[]{:S(2)}, u32[]{:S(2)}) collective-permute-start(f32[1,8,128,128]{3,2,1,0:T(8,128)S(1)} %get-tuple-element.113), channel_id=1, source_target_pairs={{0,2},{1,3},{2,0},{3,1},{4,6},{5,7},{6,4},{7,5},{8,10},{9,11},{10,... | collective-permute-start | bytes 1572872 | tf_op jit(solution)/shard_map/ppermute | solution.py:390
  158.5 14.8 %collective-permute-start.22 = (f32[1,8,128,128]{3,2,1,0:T(8,128)S(1)}, f32[1,8,128,128]{3,2,1,0:T(8,128)S(1)}, u32[]{:S(2)}, u32[]{:S(2)}) collective-permute-start(f32[1,8,128,128]{3,2,1,0:T(8,128)S(1)} %get-tuple-element.114), channel_id=1, source_target_pairs={{0,3},{1,0},{2,1},{3,2},{4,7},{5,4},{6,5},{7,6},{8,11},{9,8},{10,9... | collective-permute-start | bytes 1572872 | tf_op jit(solution)/shard_map/ppermute | solution.py:390
  166.4 32.8 %collective-permute-start.23 = (f32[4,8,128,128]{3,2,1,0:T(8,128)S(1)}, f32[4,8,128,128]{3,2,1,0:T(8,128)S(1)}, u32[]{:S(2)}, u32[]{:S(2)}) collective-permute-start(f32[4,8,128,128]{3,2,1,0:T(8,128)S(1)} %join_tiles.4), channel_id=1, source_target_pairs={{0,12},{1,13},{2,14},{3,15},{4,0},{5,1},{6,2},{7,3},{8,4},{9,5},{1... | collective-permute-start | bytes 6291464 | tf_op jit(solution)/shard_map/ppermute | solution.py:392
  174.1 47.3 %collective-permute-start.24 = (f32[4,8,128,128]{3,2,1,0:T(8,128)S(1)}, f32[4,8,128,128]{3,2,1,0:T(8,128)S(1)}, u32[]{:S(2)}, u32[]{:S(2)}) collective-permute-start(f32[4,8,128,128]{3,2,1,0:T(8,128)S(1)} %join_tiles.5), channel_id=1, source_target_pairs={{0,8},{1,9},{2,10},{3,11},{4,12},{5,13},{6,14},{7,15},{8,0},{9,1},... | collective-permute-start | bytes 6291464 | tf_op jit(solution)/shard_map/ppermute | solution.py:392
  176.4 48.6 %collective-permute-start.26 = (f32[512,512]{1,0:T(8,128)S(1)}, f32[512,512]{1,0:T(8,128)S(1)}, u32[]{:S(2)}, u32[]{:S(2)}) collective-permute-start(f32[512,512]{1,0:T(8,128)S(1)} %get-tuple-element.122), channel_id=1, source_target_pairs={{0,96},{16,112},{32,0},{48,16},{64,32},{80,48},{96,64},{112,80},{1... | collective-permute-start | bytes 3145736 | tf_op jit(solution)/shard_map/ppermute | solution.py:394
  178.4 46.6 %collective-permute-start.25 = (f32[512,512]{1,0:T(8,128)S(1)}, f32[512,512]{1,0:T(8,128)S(1)}, u32[]{:S(2)}, u32[]{:S(2)}) collective-permute-start(f32[512,512]{1,0:T(8,128)S(1)} %get-tuple-element.110), channel_id=1, source_target_pairs={{0,32},{16,48},{32,64},{48,80},{64,96},{80,112},{96,0},{112,16},{1... | collective-permute-start | bytes 3145736 | tf_op jit(solution)/shard_map/ppermute | solution.py:393
  178.4 46.1 %collective-permute-start.27 = (f32[256,512]{1,0:T(8,128)S(1)}, f32[256,512]{1,0:T(8,128)S(1)}, u32[]{:S(2)}, u32[]{:S(2)}) collective-permute-start(f32[256,512]{1,0:T(8,128)S(1)} %get-tuple-element.123), channel_id=1, source_target_pairs={{0,16},{16,0},{32,48},{48,32},{64,80},{80,64},{96,112},{112,96},{1... | collective-permute-start | bytes 1572872 | tf_op jit(solution)/shard_map/ppermute | solution.py:423
  202.3 29.4 %collective-permute-start.29 = (f32[256,512]{1,0:T(8,128)S(1)}, f32[256,512]{1,0:T(8,128)S(1)}, u32[]{:S(2)}, u32[]{:S(2)}) collective-permute-start(f32[256,512]{1,0:T(8,128)S(1)} %get-tuple-element.128), channel_id=1, source_target_pairs={{0,96},{16,112},{32,0},{48,16},{64,32},{80,48},{96,64},{112,80},{1... | collective-permute-start | bytes 1572872 | tf_op jit(solution)/shard_map/ppermute | solution.py:394
  221.4 12.6 %collective-permute-start.28 = (f32[256,512]{1,0:T(8,128)S(1)}, f32[256,512]{1,0:T(8,128)S(1)}, u32[]{:S(2)}, u32[]{:S(2)}) collective-permute-start(f32[256,512]{1,0:T(8,128)S(1)} %get-tuple-element.116), channel_id=1, source_target_pairs={{0,32},{16,48},{32,64},{48,80},{64,96},{80,112},{96,0},{112,16},{1... | collective-permute-start | bytes 1572872 | tf_op jit(solution)/shard_map/ppermute | solution.py:393
  224.5 21.9 %collective-permute-start.30 = (f32[256,512]{1,0:T(8,128)S(1)}, f32[256,512]{1,0:T(8,128)S(1)}, u32[]{:S(2)}, u32[]{:S(2)}) collective-permute-start(f32[256,512]{1,0:T(8,128)S(1)} %get-tuple-element.120), channel_id=1, source_target_pairs={{0,32},{16,48},{32,64},{48,80},{64,96},{80,112},{96,0},{112,16},{1... | collective-permute-start | bytes 1572872 | tf_op jit(solution)/shard_map/ppermute | solution.py:393
  229.3 17.2 %collective-permute-start.31 = (f32[256,512]{1,0:T(8,128)S(1)}, f32[256,512]{1,0:T(8,128)S(1)}, u32[]{:S(2)}, u32[]{:S(2)}) collective-permute-start(f32[256,512]{1,0:T(8,128)S(1)} %get-tuple-element.131), channel_id=1, source_target_pairs={{0,96},{16,112},{32,0},{48,16},{64,32},{80,48},{96,64},{112,80},{1... | collective-permute-start | bytes 1572872 | tf_op jit(solution)/shard_map/ppermute | solution.py:394
  238.8 25.5 %collective-permute-start.35 = (f32[512,512]{1,0:T(8,128)S(1)}, f32[512,512]{1,0:T(8,128)S(1)}, u32[]{:S(2)}, u32[]{:S(2)}) collective-permute-start(f32[512,512]{1,0:T(8,128)S(1)} %get-tuple-element.135), channel_id=1, source_target_pairs={{0,96},{16,112},{32,0},{48,16},{64,32},{80,48},{96,64},{112,80},{1... | collective-permute-start | bytes 3145736 | tf_op jit(solution)/shard_map/ppermute | solution.py:394
  242.6 26.5 %collective-permute-start.34 = (f32[512,512]{1,0:T(8,128)S(1)}, f32[512,512]{1,0:T(8,128)S(1)}, u32[]{:S(2)}, u32[]{:S(2)}) collective-permute-start(f32[512,512]{1,0:T(8,128)S(1)} %get-tuple-element.129), channel_id=1, source_target_pairs={{0,32},{16,48},{32,64},{48,80},{64,96},{80,112},{96,0},{112,16},{1... | collective-permute-start | bytes 3145736 | tf_op jit(solution)/shard_map/ppermute | solution.py:393
  242.6 11.5 %collective-permute-start.36 = (f32[256,512]{1,0:T(8,128)S(1)}, f32[256,512]{1,0:T(8,128)S(1)}, u32[]{:S(2)}, u32[]{:S(2)}) collective-permute-start(f32[256,512]{1,0:T(8,128)S(1)} %get-tuple-element.136), channel_id=1, source_target_pairs={{0,16},{16,0},{32,48},{48,32},{64,80},{80,64},{96,112},{112,96},{1... | collective-permute-start | bytes 1572872 | tf_op jit(solution)/shard_map/ppermute | solution.py:423
  251.2 35.5 %collective-permute-start.33 = (f32[512,512]{1,0:T(8,128)S(1)}, f32[512,512]{1,0:T(8,128)S(1)}, u32[]{:S(2)}, u32[]{:S(2)}) collective-permute-start(f32[512,512]{1,0:T(8,128)S(1)} %get-tuple-element.133), channel_id=1, source_target_pairs={{0,96},{16,112},{32,0},{48,16},{64,32},{80,48},{96,64},{112,80},{1... | collective-permute-start | bytes 3145736 | tf_op jit(solution)/shard_map/ppermute | solution.py:394
  254.1 37.5 %collective-permute-start.32 = (f32[512,512]{1,0:T(8,128)S(1)}, f32[512,512]{1,0:T(8,128)S(1)}, u32[]{:S(2)}, u32[]{:S(2)}) collective-permute-start(f32[512,512]{1,0:T(8,128)S(1)} %get-tuple-element.132), channel_id=1, source_target_pairs={{0,32},{16,48},{32,64},{48,80},{64,96},{80,112},{96,0},{112,16},{1... | collective-permute-start | bytes 3145736 | tf_op jit(solution)/shard_map/ppermute | solution.py:393
  273.3 18.2 %collective-permute-start.37 = (f32[256,512]{1,0:T(8,128)S(1)}, f32[256,512]{1,0:T(8,128)S(1)}, u32[]{:S(2)}, u32[]{:S(2)}) collective-permute-start(f32[256,512]{1,0:T(8,128)S(1)} %get-tuple-element.137), channel_id=1, source_target_pairs={{0,16},{16,0},{32,48},{48,32},{64,80},{80,64},{96,112},{112,96},{1... | collective-permute-start | bytes 1572872 | tf_op jit(solution)/shard_map/ppermute | solution.py:423
  295.8 3.2 %collective-permute-start.38 = (f32[256,512]{1,0:T(8,128)S(1)}, f32[256,512]{1,0:T(8,128)S(1)}, u32[]{:S(2)}, u32[]{:S(2)}) collective-permute-start(f32[256,512]{1,0:T(8,128)S(1)} %get-tuple-element.139), channel_id=1, source_target_pairs={{0,16},{16,0},{32,48},{48,32},{64,80},{80,64},{96,112},{112,96},{1... | collective-permute-start | bytes 1572872 | tf_op jit(solution)/shard_map/ppermute | solution.py:423
